TPU v7x, 128 devices: a whole 4x4x4 slice. The times are simulated.
128 devices in a mesh: row: 8 (over z, y_hi), col: 16 (over y_lo, x, core).
Axes of the slice: x: 4, y: 4 (y_hi: 2, y_lo: 2; y = y_hi * 2 + y_lo), z: 4, core: 2. Of those that a mesh axis runs over, the one named last changes fastest.
Arguments:
- basis_vectors: bfloat16 [8, 524288], P(None, ('row', 'col')), may hold values from -6 to 6
- block_values: bfloat16 [8, 16, 2048, 4096], P('row', 'col'), may hold values from -0.1875 to 0.1875
- blk_row: int32 [8, 16, 2048], P('row', 'col'), may hold values from 0 to 1023, as said below
- blk_col: int32 [8, 16, 2048], P('row', 'col'), may hold values from 0 to 511
- block_count: int32 [8, 16], P('row', 'col'), may hold values from 128 to 2048, as said below
Outputs:
- hx: float32 [8, 524288], P(None, ('row', 'col'))
Inputs may be any that keep to these rules, and one draw needn't show every extreme that they name: `blk_row`: in every used or unused slot the global row block is at least the global column block named by blk_col of the same slot; a pair may be named by several slots. `block_count`: some pair's count equals 2048.
All inputs are finite; a program needn't handle non-finite values.
Results may differ from a plain program's by a relative error of at most 0.0003.
Values may be sent and summed in bfloat16 or wider, within the bound.
A program may use at most 192 MiB of HBM per device.

v0:
```python
import jax
import jax.numpy as jnp
from jax import lax
from jax.sharding import PartitionSpec as P

BLK = 64
NVEC = 8


def body(basis_vectors, block_values, blk_row, blk_col, block_count):
    n_row = lax.axis_size("row")
    n_col = lax.axis_size("col")
    span_len = basis_vectors.shape[1]
    per_piece = span_len // BLK
    slot_count = block_values.shape[2]
    rank_row = lax.axis_index("row")
    rank_col = lax.axis_index("col")
    own_row = lax.all_gather(basis_vectors, "col", axis=1, tiled=True)
    own_col = lax.all_gather(basis_vectors, "row", axis=1, tiled=True)
    row_blocks = n_col * per_piece
    col_blocks = n_row * per_piece
    matrices = block_values.reshape(slot_count, BLK, BLK)
    row_index = blk_row.reshape(slot_count)
    col_index = blk_col.reshape(slot_count)
    used_slot = jnp.arange(slot_count, dtype=jnp.int32) < block_count.reshape(())
    col_vectors = jnp.take(own_col.reshape(NVEC, col_blocks, BLK), col_index, axis=1)
    row_vectors = jnp.take(own_row.reshape(NVEC, row_blocks, BLK), row_index, axis=1)
    forward = jnp.einsum("sik,vsk->vsi", matrices, col_vectors, preferred_element_type=jnp.float32)
    backward = jnp.einsum("sik,vsi->vsk", matrices, row_vectors, preferred_element_type=jnp.float32)
    row_target = jnp.where(used_slot, row_index, row_blocks)
    col_target = jnp.where(used_slot, col_index, col_blocks)
    row_terms = (
        jnp.zeros((NVEC, row_blocks, BLK), jnp.float32)
        .at[:, row_target, :]
        .add(forward, mode="drop")
    )
    col_terms = (
        jnp.zeros((NVEC, col_blocks, BLK), jnp.float32)
        .at[:, col_target, :]
        .add(backward, mode="drop")
    )
    anchor = jnp.int32(0)
    embedded = jnp.zeros((NVEC, n_row, n_col, span_len), jnp.float32)
    embedded = lax.dynamic_update_slice(
        embedded, row_terms.reshape(NVEC, 1, n_col, span_len), (anchor, rank_row, anchor, anchor)
    )
    column_slab = col_terms.reshape(NVEC, n_row, 1, span_len)
    present = lax.dynamic_slice(
        embedded, (anchor, anchor, rank_col, anchor), (NVEC, n_row, 1, span_len)
    )
    embedded = lax.dynamic_update_slice(
        embedded, present + column_slab, (anchor, anchor, rank_col, anchor)
    )
    return lax.psum_scatter(
        embedded.reshape(NVEC, n_row * n_col * span_len),
        ("row", "col"),
        scatter_dimension=1,
        tiled=True,
    )


def solution(mesh):
    return jax.shard_map(
        body,
        mesh=mesh,
        in_specs=(
            P(None, ("row", "col")),
            P("row", "col", None, None),
            P("row", "col", None),
            P("row", "col", None),
            P("row", "col"),
        ),
        out_specs=P(None, ("row", "col")),
        check_vma=False,
    )
```

profile of v0, /device:TPU:0, one launch (start us, length us, event | category | flops | bytes accessed | tf_op | source)
XLA Modules:
  0.0 1332.8 jit_solution(6849525481235721684)
XLA Ops:
  6.5 0.7 all-gather.2.cloned.1.call-update
  7.3 0.0 reduce-scatter.2.cloned.1.call-start
  7.3 38.3 %all_gather.6 = bf16[8,32768]{1,0:T(8,128)(2,1)S(1)} all-gather(bf16[8,4096]{1,0:T(8,128)(2,1)} %param.5), channel_id=1, replica_groups=mesh['row'=8,'col'=16] {'row'}, dimensions={1}, use_global_device_ids=true | all-gather | bytes 589824 | tf_op jit(solution)/shard_map/all_gather | solution.py:19
  46.2 0.7 compare_and_fusion.1
  46.9 0.8 compare_select_fusion
  47.7 1.1 reshape.148
  48.8 0.7 copy.14
  49.5 22.6 %copy.15 = bf16[1,1,2048,4096]{2,3,1,0:T(8,128)(2,1)} copy(bf16[1,1,2048,4096]{3,2,1,0:T(8,128)(2,1)} %param.6) | data formatting | bytes 33554432 | tf_op args[1]
  72.1 45.9 %copy.16 = bf16[2048,64,64]{2,1,0:T(8,128)(2,1)} copy(bf16[2048,64,64]{0,2,1:T(8,128)(2,1)} %bitcast.26) | data formatting | bytes 33554432 | tf_op jit(solution)/shard_map/reshape | solution.py:22
  118.0 14.7 %gather_fusion = bf16[2048,8,64]{2,1,0:T(8,128)(2,1)} fusion(bf16[8,512,64]{2,0,1:T(8,128)(2,1)S(1)} %copy.14, s32[2048]{0:T(1024)S(1)} %broadcast_clamp_fusion.1), kind=kCustom, calls=%fused_computation | custom fusion | bytes 4202496 | tf_op jit(solution)/shard_map/jit(_take)/gather | solution.py:26
  132.7 24.0 %fusion.2 = f32[2048,8,64]{2,1,0:T(8,128)} fusion(bf16[2048,64,64]{2,1,0:T(8,128)(2,1)} %copy.16, bf16[2048,8,64]{2,1,0:T(8,128)(2,1)} %gather_fusion, pred[2048]{0:T(1024)(128)(4,1)S(1)} %compare_and_fusion.1), kind=kOutput, calls=%fused_computation.6 | convolution fusion | flops 135266304 | bytes 23070720 | tf_op jit(solution)/shard_map/sik,vsk->vsi/dot_general | solution.py:28
  156.7 2.2 broadcast_in_dim.37
  158.9 217.7 %scatter_fusion = f32[8,1024,64]{2,0,1:T(8,128)} fusion(f32[8,1024,64]{2,0,1:T(8,128)} %broadcast_in_dim.37, s32[2048]{0:T(1024)S(1)} %bitcast.30, f32[2048,8,64]{2,1,0:T(8,128)} %fusion.2), kind=kCustom, calls=%fused_computation.2 | custom fusion | flops 1048576 | bytes 12591104 | tf_op jit(solution)/shard_map/scatter-add | solution.py:35
  376.6 5.0 copy.17
  381.6 3.7 reshape.151
  385.3 3.5 copy.18
  388.8 7.8 broadcast_in_dim.36
  396.6 39.2 %dynamic_update_slice.6 = f32[8,8,16,4096]{3,1,0,2:T(8,128)} dynamic-update-slice(f32[8,8,16,4096]{3,1,0,2:T(8,128)} %broadcast_in_dim.36, f32[8,1,16,4096]{3,1,0,2:T(1,128)S(1)} %copy-done, s32[]{:T(128)} %constant.17.clone.1, s32[]{:T(128)S(6)} %select_n.92, s32[]{:T(128)} %constant.17.clone.1, s32[]{:T(128)} %constant.17.clone.1) | dynamic-update-slice | bytes 4194308 | tf_op jit(solution)/shard_map/dynamic_update_slice | solution.py:44
  435.9 0.0 all-gather.2.cloned.1.call-done
  435.9 4.5 reshape.153
  440.4 2.9 copy.19
  443.3 14.7 %gather_fusion.1 = bf16[2048,8,64]{2,1,0:T(8,128)(2,1)} fusion(bf16[8,1024,64]{2,0,1:T(8,128)(2,1)S(1)} %copy.19, s32[2048]{0:T(1024)S(1)} %broadcast_clamp_fusion), kind=kCustom, calls=%fused_computation.1 | custom fusion | bytes 4202496 | tf_op jit(solution)/shard_map/jit(_take)/gather | solution.py:27
  458.0 19.0 %fusion = f32[2048,8,64]{2,1,0:T(8,128)} fusion(bf16[2048,64,64]{2,1,0:T(8,128)(2,1)} %copy.16, bf16[2048,8,64]{2,1,0:T(8,128)(2,1)} %gather_fusion.1, pred[2048]{0:T(1024)(128)(4,1)S(1)} %compare_and_fusion), kind=kOutput, calls=%fused_computation.4 | convolution fusion | flops 135266304 | bytes 23070720 | tf_op jit(solution)/shard_map/sik,vsi->vsk/dot_general | solution.py:29
  477.0 0.1 broadcast_in_dim.41
  477.1 142.4 %scatter_fusion.1 = f32[8,512,64]{2,0,1:T(8,128)S(1)} fusion(f32[8,512,64]{2,0,1:T(8,128)S(1)} %broadcast_in_dim.41, s32[2048]{0:T(1024)S(1)} %bitcast.29, f32[2048,8,64]{2,1,0:T(8,128)} %fusion), kind=kCustom, calls=%fused_computation.3 | custom fusion | flops 1048576 | bytes 12591104 | tf_op jit(solution)/shard_map/scatter-add | solution.py:40
  619.5 1.7 copy.21
  621.3 2.1 reshape.154
  623.4 2.3 add_dynamic-update-slice_fusion
  625.7 15.2 %copy.22 = f32[8,8,16,4096]{3,2,1,0:T(8,128)S(1)} copy(f32[8,8,16,4096]{3,1,0,2:T(8,128)} %add_dynamic-update-slice_fusion) | data formatting | bytes 33554432 | tf_op jit(solution)/shard_map/dynamic_update_slice | solution.py:51
  640.9 19.3 %copy.23 = f32[1,8,128,4096]{3,1,2,0:T(8,128)} copy(f32[1,8,128,4096]{3,2,1,0:T(8,128)S(1)} %bitcast.28) | data formatting | bytes 33554432
  660.3 0.0 reduce-scatter.2.cloned.1.call-update
  660.3 665.7 %reduce-scatter.2.cloned.1.call-done = f32[8,4096]{1,0:T(8,128)} async-done(((f32[8,524288]{1,0:T(8,128)}), f32[8,4096]{1,0:T(8,128)}) %reduce-scatter.2.cloned.1.call-update) | async-done | bytes 131088 | tf_op jit(solution)/shard_map/reduce_scatter | solution.py:54
  (8 shorter events, 0.0 us)
Async XLA Ops:
  6.5 429.4 %all-gather.2.cloned.1.call-start = ((), (), s32[]{:S(2)}) async-start(), calls=%async_computation.1 | async-start | bytes 1114112 | tf_op jit(solution)/shard_map/all_gather | solution.py:18
  7.3 1318.7 %reduce-scatter.2.cloned.1.call-start = ((), (), s32[]{:S(2)}) async-start(), calls=%async_computation.2 | async-start | bytes 16908288 | tf_op jit(solution)/shard_map/reduce_scatter | solution.py:54
  388.8 7.8 copy-start
  396.6 39.2 %copy-start.1 = (s32[1,1,2048]{2,1,0:T(1,128)S(1)}, s32[1,1,2048]{2,1,0:T(1,128)}, u32[]{:S(2)}) copy-start(s32[1,1,2048]{2,1,0:T(1,128)} %param.7) | copy-start | bytes 24580
Sparse Core Ops, SparseCore 0:
  9.1 35.1 all-gather.1
  660.4 665.5 reduce-scatter.1
where the time goes:
time: 1350 us; the launch traced here: 1330 us
  waiting for transfers between devices  666 us (49%)
  other arithmetic  364 us (27%)
  local copies, waits for them, and re-layouts  207 us (15%)
  matrix products  43 us (3%)
  blocking collectives  38.3 us (3%)
  between operations  14.1 us (1%)
    reduce_scatter x1, waiting for transfers between devices, body(): lax.psum_scatter(embedded.reshape(NVEC, n_row * n_col * span_len), ('row'...  666 us
    scatter-add x1, other arithmetic, body(): row_terms = jnp.zeros((NVEC, row_blocks, BLK), jnp.float32).at[:, row_tar...  218 us
    scatter-add x1, other arithmetic, body(): col_terms = jnp.zeros((NVEC, col_blocks, BLK), jnp.float32).at[:, col_tar...  142 us
    reshape x1, local copies, waits for them, and re-layouts, body(): matrices = block_values.reshape(slot_count, BLK, BLK)  45.9 us
    unnamed x6, local copies, waits for them, and re-layouts  41.9 us
    dynamic_update_slice x1, local copies, waits for them, and re-layouts, body(): lax.dynamic_update_slice(embedded, row_terms.reshape(NVEC, 1, n_col, span...  39.2 us
    all_gather x1, blocking collectives, body(): own_col = lax.all_gather(basis_vectors, 'row', axis=1, tiled=True)  38.3 us
  transfers between devices with their start and end apart: 2, of which 1 were waited for; matrix products, arithmetic and copies ran while one was open for 29% of the time, Pallas kernels for 0%

commit v1 on v0

v1 whole, which is shorter than its diff:
```python
import jax
import jax.numpy as jnp
from jax import lax
from jax.experimental import pallas as pl
from jax.experimental.pallas import tpu as pltpu
from jax.sharding import PartitionSpec as P

BLK = 64
NVEC = 8
PIECE = 4096
CAP = 2048
N_ROW = 8
N_COL = 16
NB_ROW = 1024
NB_COL = 512
GROUPS = CAP // 8
UNROLL = 8
F32, BF16 = jnp.float32, jnp.bfloat16
MESH = pl.DeviceIdType.MESH
SMEM = pl.BlockSpec(memory_space=pltpu.SMEM)
VMEM = pl.BlockSpec(memory_space=pltpu.VMEM)
ANY = pl.BlockSpec(memory_space=pl.ANY)
MIB = 2**20


def lane_masks():
    lane = lax.broadcasted_iota(jnp.int32, (8, 128), 1)
    return lane < 64, lane % 2 == 0


class Place:
    def __init__(self):
        self.row, self.col = lax.axis_index("row"), lax.axis_index("col")
        self.z, self.yh = self.row // 2, self.row % 2
        self.yl, self.x, self.core = self.col // 8, (self.col // 2) % 4, self.col % 2
        self.sibling = (self.row, self.col_of(self.yl, self.x, 1 - self.core))
        self.y_lo = (self.row, self.col_of(1 - self.yl, self.x, self.core))
        self.y_hi = (self.row_of(self.z, 1 - self.yh), self.col)
        self.xs = [(self.row, self.col_of(self.yl, (self.x + d) % 4, self.core)) for d in (1, 2, 3)]
        self.zs = [(self.row_of((self.z + d) % 4, self.yh), self.col) for d in (1, 2, 3)]
        self.partners = [self.sibling, self.y_lo, self.y_hi] + self.xs + self.zs

    def col_of(self, yl, x, core):
        return (yl * 4 + x) * 2 + core

    def row_of(self, z, yh):
        return z * 2 + yh

    def greet(self):
        barrier = pltpu.get_barrier_semaphore()
        for partner in self.partners:
            pl.semaphore_signal(barrier, inc=1, device_id=partner, device_id_type=MESH)

    def wait_greetings(self):
        pl.semaphore_wait(pltpu.get_barrier_semaphore(), len(self.partners))


class Sender:
    def __init__(self, sems):
        self.sems, self.sent = sems, []

    def send(self, src, dst, recv_sem, to):
        copy = pltpu.make_async_remote_copy(
            src_ref=src, dst_ref=dst, send_sem=self.sems.at[len(self.sent)], recv_sem=recv_sem,
            device_id=to, device_id_type=MESH)
        copy.start()
        self.sent.append(copy)

    def arrived(self, dst, recv_sem, place):
        pltpu.make_async_remote_copy(
            src_ref=dst, dst_ref=dst, send_sem=self.sems.at[0], recv_sem=recv_sem,
            device_id=place.sibling, device_id_type=MESH).wait_recv()

    def finish(self):
        for copy in self.sent:
            copy.wait_send()


def expand_row(src, ex, piece):
    low, even = lane_masks()

    def step(i, carry):
        for j in range(8):
            m = i * 8 + j
            x = src[:, pl.ds(pl.multiple_of(m * 128, 128), 128)].astype(F32)
            swapped = pltpu.roll(x, 64, 1)
            for h in range(2):
                d = jnp.where(low, x, swapped) if h == 0 else jnp.where(low, swapped, x)
                p0 = jnp.where(even, d, pltpu.roll(d, 1, 1))
                p1 = jnp.where(even, pltpu.roll(d, 127, 1), d)
                ex[piece * 64 + 2 * m + h] = jnp.concatenate([p0, p1], axis=0).astype(BF16)
        return carry

    lax.fori_loop(0, 4, step, 0)


def expand_col(src, xc, piece):
    low, _ = lane_masks()

    def step(i, carry):
        for j in range(8):
            m = i * 8 + j
            x = src[:, pl.ds(pl.multiple_of(m * 128, 128), 128)].astype(F32)
            swapped = pltpu.roll(x, 64, 1)
            zero = jnp.zeros_like(x)
            xc[piece * 64 + 2 * m] = jnp.concatenate([jnp.where(low, x, zero), jnp.where(low, zero, swapped)], axis=0).astype(BF16)
            xc[piece * 64 + 2 * m + 1] = jnp.concatenate([jnp.where(low, swapped, zero), jnp.where(low, zero, x)], axis=0).astype(BF16)
        return carry

    lax.fori_loop(0, 4, step, 0)


def gather_kernel(x_ref, val_ref, ex, xc, vals, racc, cacc, rowx, colx, val_sem, send_sem, row_sem, col_sem):
    place = Place()
    loads = [pltpu.make_async_copy(val_ref.at[:, :, q], vals.at[:, q], val_sem.at[q]) for q in range(4)]
    for load in loads:
        load.start()
    place.greet()
    place.wait_greetings()
    out = Sender(send_sem)
    me_c, me_r = place.col, place.row
    out.send(x_ref, rowx.at[me_c], row_sem.at[me_c], place.y_lo)
    out.send(x_ref, colx.at[me_r], col_sem.at[me_r], place.y_hi)
    for to in place.xs:
        out.send(x_ref, rowx.at[me_c], row_sem.at[me_c], to)
    for to in place.zs:
        out.send(x_ref, colx.at[me_r], col_sem.at[me_r], to)
    out.send(x_ref, rowx.at[me_c], row_sem.at[me_c], place.sibling)
    expand_row(x_ref, ex, me_c)
    expand_col(x_ref, xc, me_r)

    def zero_rows(i, carry):
        racc[pl.ds(i * 16, 16)] = jnp.zeros((16, 16, 128), F32)
        return carry

    lax.fori_loop(0, NB_ROW // 16, zero_rows, 0)

    def zero_cols(i, carry):
        cacc[pl.ds(i * 16, 16)] = jnp.zeros((16, 8, 128), F32)
        return carry

    lax.fori_loop(0, NB_COL // 16, zero_cols, 0)

    def take_row(slot, targets):
        out.arrived(rowx.at[slot], row_sem.at[slot], place)
        for to in targets:
            out.send(rowx.at[slot], rowx.at[slot], row_sem.at[slot], to)
        expand_row(rowx.at[slot], ex, slot)

    def take_col(slot, targets):
        out.arrived(colx.at[slot], col_sem.at[slot], place)
        for to in targets:
            out.send(colx.at[slot], colx.at[slot], col_sem.at[slot], to)
        expand_col(colx.at[slot], xc, slot)

    yl, x, core, z, yh = place.yl, place.x, place.core, place.z, place.yh
    take_row(place.y_lo[1], place.xs + [place.sibling])
    take_col(place.y_hi[0], place.zs)
    for d in (1, 3, 2):
        take_row(place.col_of(yl, (x + d) % 4, core), [place.sibling])
        take_col(place.row_of((z + d) % 4, yh), [])
    for d in (1, 3, 2):
        take_row(place.col_of(1 - yl, (x + d) % 4, core), [place.sibling])
        take_col(place.row_of((z + d) % 4, 1 - yh), [])
    for d in (0, 1, 3, 2):
        take_row(place.col_of(yl, (x + d) % 4, 1 - core), [])
        take_row(place.col_of(1 - yl, (x + d) % 4, 1 - core), [])
    out.finish()
    for load in loads:
        load.wait()


def gather(basis_vectors, block_values):
    pairs = block_values.reshape(GROUPS, 4, 2, 32, 128).transpose(0, 3, 1, 2, 4)
    ex, xc, vals, racc, cacc = pl.pallas_call(
        gather_kernel,
        out_shape=(
            pltpu.VMEM((NB_ROW, 16, 128), BF16),
            pltpu.VMEM((NB_COL, 16, 128), BF16),
            pltpu.VMEM((GROUPS, 4, 32, 2, 128), BF16),
            pltpu.VMEM((NB_ROW + 1, 16, 128), F32),
            pltpu.VMEM((NB_COL + 1, 8, 128), F32),
        ),
        in_specs=[VMEM, ANY],
        out_specs=(VMEM,) * 5,
        scratch_shapes=[
            pltpu.VMEM((N_COL, NVEC, PIECE), BF16),
            pltpu.VMEM((N_ROW, NVEC, PIECE), BF16),
            pltpu.SemaphoreType.DMA((4,)),
            pltpu.SemaphoreType.DMA((23,)),
            pltpu.SemaphoreType.DMA((N_COL,)),
            pltpu.SemaphoreType.DMA((N_ROW,)),
        ],
        compiler_params=pltpu.CompilerParams(collective_id=0, has_side_effects=True, vmem_limit_bytes=8 * MIB),
    )(basis_vectors, pairs)
    return ex, xc, vals.reshape(GROUPS, 256, 128), racc, cacc


def product_kernel(count_ref, row_index, col_index, ex, xc, vals, racc_in, cacc_in, racc, cacc):
    count = count_ref[0]
    low, _ = lane_masks()
    lane = lax.broadcasted_iota(jnp.int32, (16, 128), 1)
    mine = [(lane // 64 == i // 2) & (lane % 2 == i % 2) for i in range(4)]
    weight = [jnp.where(m, 1.0, 0.0).astype(BF16) for m in mine]

    def group(t, guarded):
        base = t * 8
        rows = [row_index[base + s] for s in range(8)]
        cols = [col_index[base + s] for s in range(8)]
        to_rows, to_cols = rows, cols
        if guarded:
            to_rows = [jnp.where(base + s < count, rows[s], NB_ROW) for s in range(8)]
            to_cols = [jnp.where(base + s < count, cols[s], NB_COL) for s in range(8)]
        for h in range(2):
            a = vals[t, h * 128:(h + 1) * 128, :]
            left = jnp.concatenate([xc[cols[4 * h + i]] for i in range(4)], axis=0)
            right = jnp.concatenate([ex[rows[4 * h + i]] * weight[i] for i in range(4)], axis=0)
            forward = lax.dot_general(left, a, (((1,), (1,)), ((), ())), preferred_element_type=F32)
            backward = lax.dot_general(right, a, (((1,), (0,)), ((), ())), preferred_element_type=F32)
            for i in range(4):
                racc[to_rows[4 * h + i]] += jnp.where(mine[i], forward[i * 16:(i + 1) * 16], 0.0)
                cacc[to_cols[4 * h + i]] += jnp.where(low, backward[i * 16:i * 16 + 8], backward[i * 16 + 8:i * 16 + 16])

    whole = count // (8 * UNROLL)

    def fast(u, carry):
        for k in range(UNROLL):
            group(u * UNROLL + k, False)
        return carry

    lax.fori_loop(0, whole, fast, 0)

    def slow(t, carry):
        group(t, True)
        return carry

    lax.fori_loop(whole * UNROLL, (count + 7) // 8, slow, 0)


def products(count, row_index, col_index, ex, xc, vals, racc, cacc):
    return pl.pallas_call(
        product_kernel,
        out_shape=(pltpu.VMEM((NB_ROW + 1, 16, 128), F32), pltpu.VMEM((NB_COL + 1, 8, 128), F32)),
        in_specs=[SMEM, SMEM, SMEM, VMEM, VMEM, VMEM, VMEM, VMEM],
        out_specs=(VMEM, VMEM),
        input_output_aliases={6: 0, 7: 1},
        compiler_params=pltpu.CompilerParams(vmem_limit_bytes=4 * MIB),
    )(count, row_index, col_index, ex, xc, vals, racc, cacc)


def fold_row(racc, piece, put):
    low, even = lane_masks()

    def step(i, carry):
        for j in range(8):
            m = i * 8 + j
            ae, ao = racc[piece * 64 + 2 * m], racc[piece * 64 + 2 * m + 1]
            z = []
            for p in range(2):
                e, o = ae[p * 8:p * 8 + 8], ao[p * 8:p * 8 + 8]
                z.append(jnp.where(low, e, o) + pltpu.roll(jnp.where(low, o, e), 64, 1))
            w = jnp.where(even, z[1], z[0])
            y = jnp.where(even, z[0], z[1]) + jnp.where(even, pltpu.roll(w, 127, 1), pltpu.roll(w, 1, 1))
            put(pl.ds(pl.multiple_of(m * 128, 128), 128), y)
        return carry

    lax.fori_loop(0, 4, step, 0)


def fold_col(cacc, piece, put):
    low, _ = lane_masks()

    def step(i, carry):
        for j in range(8):
            m = i * 8 + j
            e, o = cacc[piece * 64 + 2 * m], cacc[piece * 64 + 2 * m + 1]
            put(pl.ds(pl.multiple_of(m * 128, 128), 128), jnp.where(low, e, o) + pltpu.roll(jnp.where(low, o, e), 64, 1))
        return carry

    lax.fori_loop(0, 4, step, 0)


def add_up(dst, terms):
    def step(i, carry):
        at = pl.ds(pl.multiple_of(i * 512, 512), 512)
        total = terms[0][:, at]
        for term in terms[1:]:
            total = total + term[:, at]
        dst[:, at] = total
        return carry

    lax.fori_loop(0, PIECE // 512, step, 0)


def scatter_kernel(racc, cacc, out_ref, for_core, from_core, row_part, from_x, row_sum, from_ylo,
                   col_part, from_z, col_sum, from_yhi, send_sem, core_sem, x_sem, ylo_sem, z_sem, yhi_sem):
    place = Place()
    place.greet()
    yl, x, core, z, yh = place.yl, place.x, place.core, place.z, place.yh
    out = Sender(send_sem)

    def write(ref):
        def put(at, y):
            ref[:, at] = y
        return put

    first = True
    for d in (1, 3, 2):
        for h in (1, 0):
            hh = 1 - yh if h else yh
            fold_col(cacc, place.row_of((z + d) % 4, hh), write(col_part.at[d, h]))
            if first:
                place.wait_greetings()
                first = False
            out.send(col_part.at[d, h], from_z.at[d - 1, h], z_sem.at[d - 1, h], place.zs[d - 1])
    for d in (1, 3, 2, 0):
        for h in (1, 0):
            hh = 1 - yl if h else yl
            fold_row(racc, place.col_of(hh, (x + d) % 4, 1 - core), write(for_core.at[d, h]))
            out.send(for_core.at[d, h], from_core.at[d, h], core_sem.at[d, h], place.sibling)
    for h in (1, 0):
        hh = 1 - yh if h else yh
        fold_col(cacc, place.row_of(z, hh), write(col_part.at[0, h]))
    for d in (1, 3, 2, 0):
        for h in (1, 0):
            hh = 1 - yl if h else yl
            out.arrived(from_core.at[d, h], core_sem.at[d, h], place)

            def put(at, y, d=d, h=h):
                row_part[d, h, :, at] = y + from_core[d, h, :, at]

            fold_row(racc, place.col_of(hh, (x + d) % 4, core), put)
            if d:
                out.send(row_part.at[d, h], from_x.at[d - 1, h], x_sem.at[d - 1, h], place.xs[d - 1])
    for d in (1, 3, 2):
        out.arrived(from_z.at[d - 1, 1], z_sem.at[d - 1, 1], place)
    add_up(col_sum.at[1], [col_part.at[0, 1]] + [from_z.at[k, 1] for k in range(3)])
    out.send(col_sum.at[1], from_yhi, yhi_sem.at[0], place.y_hi)
    for d in (1, 3, 2):
        out.arrived(from_x.at[d - 1, 1], x_sem.at[d - 1, 1], place)
    add_up(row_sum.at[1], [row_part.at[0, 1]] + [from_x.at[k, 1] for k in range(3)])
    out.send(row_sum.at[1], from_ylo, ylo_sem.at[0], place.y_lo)
    for d in (1, 3, 2):
        out.arrived(from_z.at[d - 1, 0], z_sem.at[d - 1, 0], place)
        out.arrived(from_x.at[d - 1, 0], x_sem.at[d - 1, 0], place)
    add_up(row_sum.at[0], [row_part.at[0, 0], col_part.at[0, 0]] + [from_x.at[k, 0] for k in range(3)] + [from_z.at[k, 0] for k in range(3)])
    out.arrived(from_yhi, yhi_sem.at[0], place)
    out.arrived(from_ylo, ylo_sem.at[0], place)
    add_up(out_ref, [row_sum.at[0], from_yhi, from_ylo])
    out.finish()


def scatter(racc, cacc):
    piece = (NVEC, PIECE)
    return pl.pallas_call(
        scatter_kernel,
        out_shape=jax.ShapeDtypeStruct(piece, F32),
        in_specs=[VMEM, VMEM],
        out_specs=VMEM,
        scratch_shapes=[
            pltpu.VMEM((4, 2) + piece, F32), pltpu.VMEM((4, 2) + piece, F32),
            pltpu.VMEM((4, 2) + piece, F32), pltpu.VMEM((3, 2) + piece, F32),
            pltpu.VMEM((2,) + piece, F32), pltpu.VMEM(piece, F32),
            pltpu.VMEM((4, 2) + piece, F32), pltpu.VMEM((3, 2) + piece, F32),
            pltpu.VMEM((2,) + piece, F32), pltpu.VMEM(piece, F32),
            pltpu.SemaphoreType.DMA((22,)),
            pltpu.SemaphoreType.DMA((4, 2)), pltpu.SemaphoreType.DMA((3, 2)), pltpu.SemaphoreType.DMA((1,)),
            pltpu.SemaphoreType.DMA((3, 2)), pltpu.SemaphoreType.DMA((1,)),
        ],
        compiler_params=pltpu.CompilerParams(collective_id=1, has_side_effects=True, vmem_limit_bytes=8 * MIB),
    )(racc, cacc)


def body(basis_vectors, block_values, blk_row, blk_col, block_count):
    ex, xc, vals, racc, cacc = gather(basis_vectors, block_values.reshape(CAP, BLK * BLK))
    racc, cacc = products(block_count.reshape(1), blk_row.reshape(CAP), blk_col.reshape(CAP), ex, xc, vals, racc, cacc)
    return scatter(racc, cacc)


def solution(mesh):
    return jax.shard_map(
        body,
        mesh=mesh,
        in_specs=(
            P(None, ("row", "col")),
            P("row", "col", None, None),
            P("row", "col", None),
            P("row", "col", None),
            P("row", "col"),
        ),
        out_specs=P(None, ("row", "col")),
        check_vma=False,
    )
```

time: 1350 us -> 69.5 us (0.05); the launches traced: 1330 us -> 69 us
  waiting for transfers between devices: 666 us -> 0 us
  other arithmetic: 364 us -> 0 us
  local copies, waits for them, and re-layouts: 207 us -> 1.5 us
  Pallas kernels: 0 us -> 66.8 us
  matrix products: 43 us -> 0 us
  blocking collectives: 38.3 us -> 0 us
    reduce_scatter x1 -> x0, waiting for transfers between devices: 666 us -> none  [body(): lax.psum_scatter(embedded.reshape(NVEC, n_row * n_col * span_len), ('row'...]
    scatter-add x2 -> x0, other arithmetic: 360 us -> none  [the longest x1 218 us: body(): row_terms = jnp.zeros((NVEC, row_blocks, BLK), jnp.float32).at[:, row_tar...]
    pallas_call x0 -> x3, Pallas kernels: none -> 66.8 us  [the longest x1 33.6 us: scatter(): pl.pallas_call(scatter_kernel, out_shape=jax.ShapeDtypeStruct(piece, F32)...]
    reshape x8 -> x0, local copies, waits for them, and re-layouts: 64.4 us -> none  [the longest x1 45.9 us: body(): matrices = block_values.reshape(slot_count, BLK, BLK)]
    dynamic_update_slice x2 -> x0, local copies, waits for them, and re-layouts: 54.4 us -> none  [the longest x1 39.2 us: body(): lax.dynamic_update_slice(embedded, row_terms.reshape(NVEC, 1, n_col, span...]
    dot_general x2 -> x0, matrix products: 43 us -> none  [the longest x1 24 us: body(): jnp.einsum('sik,vsk->vsi', matrices, col_vectors, preferred_element_type=...]
    unnamed x6 -> x7, local copies, waits for them, and re-layouts: 41.9 us -> 1.5 us
    all_gather x1 -> x0, blocking collectives: 38.3 us -> none  [body(): own_col = lax.all_gather(basis_vectors, 'row', axis=1, tiled=True)]
  transfers between devices with their start and end apart: 2 -> 0, of which waited for: 1 -> 0; matrix products, arithmetic and copies ran while one was open for 29% -> 0% of each run, Pallas kernels for 0% -> 0%
where the time goes in v1:
time: 69.5 us; the launch traced here: 69 us
  Pallas kernels  66.8 us (96%)
  local copies, waits for them, and re-layouts  1.5 us (2%)
  between operations  0.7 us (1%)
    pallas_call x1, Pallas kernels, scatter(): pl.pallas_call(scatter_kernel, out_shape=jax.ShapeDtypeStruct(piece, F32)...  33.6 us
    pallas_call x1, Pallas kernels, gather(): pl.pallas_call(gather_kernel, out_shape=(pltpu.VMEM((NB_ROW, 16, 128), BF...  23.4 us
    pallas_call x1, Pallas kernels, products(): pl.pallas_call(product_kernel, out_shape=(pltpu.VMEM((NB_ROW + 1, 16, 128...  9.8 us
    unnamed x7, local copies, waits for them, and re-layouts  1.5 us

profile of v1, /device:TPU:0, one launch (start us, length us, event | category | flops | bytes accessed | tf_op | source)
XLA Modules:
  0.0 69.0 jit_solution(11535194820110947294)
XLA Ops:
  0.7 0.0 copy-start
  0.7 0.8 %copy-done = bf16[8,4096]{1,0:T(8,128)(2,1)S(1)} copy-done((bf16[8,4096]{1,0:T(8,128)(2,1)S(1)}, bf16[8,4096]{1,0:T(8,128)(2,1)}, u32[]{:S(2)}) %copy-start) | copy-done | bytes 65560
  1.5 0.0 copy-start.1
  1.5 0.0 copy-start.2
  1.5 23.4 %shard_map.55 = (bf16[1024,16,128]{2,1,0:T(8,128)(2,1)S(1)}, bf16[512,16,128]{2,1,0:T(8,128)(2,1)S(1)}, bf16[256,4,32,2,128]{4,3,2,1,0:T(2,128)(2,1)S(1)}, f32[1...) custom-call(bf16[8,4096]{1,0:T(8,128)(2,1)S(1)} %copy-done, bf16[256,32,4,2,128]{4,3,2,1,0:T(2,128)(2,1)} %bitcast.11), custom_call_target="tpu_custom_call" | custom-call | tf_op jit(solution)/shard_map/pallas_call | solution.py:175
  24.9 0.0 copy-done.1
  24.9 0.0 copy-done.2
  24.9 9.8 %shard_map.56 = (f32[1025,16,128]{2,1,0:T(8,128)S(1)}, f32[513,8,128]{2,1,0:T(8,128)S(1)}) custom-call(s32[1]{0:T(128)} %bitcast.7.count_ref, s32[2048]{0:T(1024)S(1)} %bitcast.9, s32[2048]{0:T(1024)S(1)} %bitcast.10, bf16[1024,16,128]{2,1,0:T(8,128)(2,1)S(1)} %get-tuple-element.12.ex, ...), custom_call_target="tpu_custom_call", output_to_operand_aliasing={{0}: (6, {}), {1}: (7, {})} | custom-call | tf_op jit(solution)/shard_map/pallas_call | solution.py:241
  34.7 33.6 %shard_map.57 = f32[8,4096]{1,0:T(8,128)S(1)} custom-call(f32[1025,16,128]{2,1,0:T(8,128)S(1)} %get-tuple-element.17.racc, f32[513,8,128]{2,1,0:T(8,128)S(1)} %get-tuple-element.18.cacc), custom_call_target="tpu_custom_call" | custom-call | tf_op jit(solution)/shard_map/pallas_call | solution.py:355
  68.3 0.7 copy.12
Async XLA Ops:
  0.7 0.8 %copy-start = (bf16[8,4096]{1,0:T(8,128)(2,1)S(1)}, bf16[8,4096]{1,0:T(8,128)(2,1)}, u32[]{:S(2)}) copy-start(bf16[8,4096]{1,0:T(8,128)(2,1)} %x_ref.1) | copy-start | bytes 196612
  1.5 23.4 %copy-start.1 = (s32[1,1,2048]{2,1,0:T(1,128)S(1)}, s32[1,1,2048]{2,1,0:T(1,128)}, u32[]{:S(2)}) copy-start(s32[1,1,2048]{2,1,0:T(1,128)} %param.7) | copy-start | bytes 24580
  1.5 23.4 %copy-start.2 = (s32[1,1,2048]{2,1,0:T(1,128)S(1)}, s32[1,1,2048]{2,1,0:T(1,128)}, u32[]{:S(2)}) copy-start(s32[1,1,2048]{2,1,0:T(1,128)} %param.8) | copy-start | bytes 24580

commit v2 on v1

v2 whole, which is shorter than its diff:
```python
import jax
import jax.numpy as jnp
from jax import lax
from jax.experimental import pallas as pl
from jax.experimental.pallas import tpu as pltpu
from jax.sharding import PartitionSpec as P

BLK = 64
NVEC = 8
PIECE = 4096
CAP = 2048
N_ROW = 8
N_COL = 16
NB_ROW = 1024
NB_COL = 512
GROUPS = CAP // 8
UNROLL = 32
TOP = 32767.0
F32, BF16, I16, I32 = jnp.float32, jnp.bfloat16, jnp.int16, jnp.int32
MESH = pl.DeviceIdType.MESH
SMEM = pl.BlockSpec(memory_space=pltpu.SMEM)
VMEM = pl.BlockSpec(memory_space=pltpu.VMEM)
ANY = pl.BlockSpec(memory_space=pl.ANY)
MIB = 2**20


def lane_masks():
    lane = lax.broadcasted_iota(jnp.int32, (8, 128), 1)
    return lane < 64, lane % 2 == 0


class Place:
    def __init__(self):
        self.row, self.col = lax.axis_index("row"), lax.axis_index("col")
        self.z, self.yh = self.row // 2, self.row % 2
        self.yl, self.x, self.core = self.col // 8, (self.col // 2) % 4, self.col % 2
        self.sibling = (self.row, self.col_of(self.yl, self.x, 1 - self.core))
        self.y_lo = (self.row, self.col_of(1 - self.yl, self.x, self.core))
        self.y_hi = (self.row_of(self.z, 1 - self.yh), self.col)
        self.xs = [(self.row, self.col_of(self.yl, (self.x + d) % 4, self.core)) for d in (1, 2, 3)]
        self.zs = [(self.row_of((self.z + d) % 4, self.yh), self.col) for d in (1, 2, 3)]
        self.partners = [self.sibling, self.y_lo, self.y_hi] + self.xs + self.zs

    def col_of(self, yl, x, core):
        return (yl * 4 + x) * 2 + core

    def row_of(self, z, yh):
        return z * 2 + yh

    def greet(self):
        barrier = pltpu.get_barrier_semaphore()
        for partner in self.partners:
            pl.semaphore_signal(barrier, inc=1, device_id=partner, device_id_type=MESH)

    def wait_greetings(self):
        pl.semaphore_wait(pltpu.get_barrier_semaphore(), len(self.partners))


class Sender:
    def __init__(self, sems):
        self.sems, self.sent = sems, []

    def send(self, src, dst, recv_sem, to):
        copy = pltpu.make_async_remote_copy(
            src_ref=src, dst_ref=dst, send_sem=self.sems.at[len(self.sent)], recv_sem=recv_sem,
            device_id=to, device_id_type=MESH)
        copy.start()
        self.sent.append(copy)

    def arrived(self, dst, recv_sem, place):
        pltpu.make_async_remote_copy(
            src_ref=dst, dst_ref=dst, send_sem=self.sems.at[0], recv_sem=recv_sem,
            device_id=place.sibling, device_id_type=MESH).wait_recv()

    def finish(self):
        for copy in self.sent:
            copy.wait_send()


def block_rows(block):
    return pl.ds(pl.multiple_of(block * 8, 8), 8)


def lane_tile(m):
    return pl.ds(pl.multiple_of(m * 128, 128), 128)


def expand(src, dst, piece):
    low, _ = lane_masks()

    def step(i, carry):
        for j in range(16):
            m = i * 16 + j
            x = src[:, lane_tile(m)].astype(F32)
            swapped = pltpu.roll(x, 64, 1)
            dst[block_rows(piece * 64 + 2 * m), :] = jnp.where(low, x, swapped)
            dst[block_rows(piece * 64 + 2 * m + 1), :] = jnp.where(low, swapped, x)
        return carry

    lax.fori_loop(0, 2, step, 0)


def gather_kernel(count_ref, row_index, col_index, x_ref, val_ref, ex, xc, vals, racc, cacc, to_rows, to_cols, rowx, colx, val_sem, send_sem, row_sem, col_sem):
    place = Place()
    loads = [pltpu.make_async_copy(val_ref.at[:, :, q], vals.at[:, q], val_sem.at[q]) for q in range(4)]
    for load in loads:
        load.start()
    place.greet()
    place.wait_greetings()
    out = Sender(send_sem)
    me_c, me_r = place.col, place.row
    out.send(x_ref, rowx.at[me_c], row_sem.at[me_c], place.y_lo)
    out.send(x_ref, colx.at[me_r], col_sem.at[me_r], place.y_hi)
    for to in place.xs:
        out.send(x_ref, rowx.at[me_c], row_sem.at[me_c], to)
    for to in place.zs:
        out.send(x_ref, colx.at[me_r], col_sem.at[me_r], to)
    out.send(x_ref, rowx.at[me_c], row_sem.at[me_c], place.sibling)
    expand(x_ref, ex, me_c)
    expand(x_ref, xc, me_r)
    slot = lax.broadcasted_iota(I32, (16, 128), 0) * 128 + lax.broadcasted_iota(I32, (16, 128), 1)
    used = slot < count_ref[0]
    to_rows[...] = jnp.where(used, row_index[...], NB_ROW) * 8
    to_cols[...] = jnp.where(used, col_index[...], NB_COL) * 8
    spare = jnp.zeros((8, 128), F32)
    ex[block_rows(NB_ROW), :] = spare
    xc[block_rows(NB_COL), :] = spare

    def zero_rows(i, carry):
        at = pl.ds(pl.multiple_of(i * 128, 128), 128)
        racc[:, at, :] = jnp.zeros((2, 128, 128), F32)
        return carry

    lax.fori_loop(0, NB_ROW * 8 // 128, zero_rows, 0)

    def zero_cols(i, carry):
        cacc[pl.ds(pl.multiple_of(i * 128, 128), 128), :] = jnp.zeros((128, 128), F32)
        return carry

    lax.fori_loop(0, NB_COL * 8 // 128, zero_cols, 0)

    def take_row(slot, targets):
        out.arrived(rowx.at[slot], row_sem.at[slot], place)
        for to in targets:
            out.send(rowx.at[slot], rowx.at[slot], row_sem.at[slot], to)
        expand(rowx.at[slot], ex, slot)

    def take_col(slot, targets):
        out.arrived(colx.at[slot], col_sem.at[slot], place)
        for to in targets:
            out.send(colx.at[slot], colx.at[slot], col_sem.at[slot], to)
        expand(colx.at[slot], xc, slot)

    yl, x, core, z, yh = place.yl, place.x, place.core, place.z, place.yh
    take_row(place.y_lo[1], place.xs + [place.sibling])
    take_col(place.y_hi[0], place.zs)
    for d in (1, 3, 2):
        take_row(place.col_of(yl, (x + d) % 4, core), [place.sibling])
        take_col(place.row_of((z + d) % 4, yh), [])
    for d in (1, 3, 2):
        take_row(place.col_of(1 - yl, (x + d) % 4, core), [place.sibling])
        take_col(place.row_of((z + d) % 4, 1 - yh), [])
    for d in (0, 1, 3, 2):
        take_row(place.col_of(yl, (x + d) % 4, 1 - core), [])
        take_row(place.col_of(1 - yl, (x + d) % 4, 1 - core), [])
    out.finish()
    for load in loads:
        load.wait()


def gather(count, row_index, col_index, basis_vectors, block_values):
    pairs = block_values.reshape(GROUPS, 4, 2, 32, 128).transpose(0, 3, 1, 2, 4)
    ex, xc, vals, racc, cacc, to_rows, to_cols = pl.pallas_call(
        gather_kernel,
        out_shape=(
            pltpu.VMEM(((NB_ROW + 1) * 8, 128), F32),
            pltpu.VMEM(((NB_COL + 1) * 8, 128), F32),
            pltpu.VMEM((GROUPS, 4, 32, 2, 128), BF16),
            pltpu.VMEM((2, (NB_ROW + 1) * 8, 128), F32),
            pltpu.VMEM(((NB_COL + 1) * 8, 128), F32),
            pltpu.VMEM((16, 128), I32),
            pltpu.VMEM((16, 128), I32),
        ),
        in_specs=[SMEM, VMEM, VMEM, VMEM, ANY],
        out_specs=(VMEM,) * 7,
        scratch_shapes=[
            pltpu.VMEM((N_COL, NVEC, PIECE), BF16),
            pltpu.VMEM((N_ROW, NVEC, PIECE), BF16),
            pltpu.SemaphoreType.DMA((4,)),
            pltpu.SemaphoreType.DMA((23,)),
            pltpu.SemaphoreType.DMA((N_COL,)),
            pltpu.SemaphoreType.DMA((N_ROW,)),
        ],
        compiler_params=pltpu.CompilerParams(collective_id=0, has_side_effects=True, vmem_limit_bytes=8 * MIB),
    )(count, row_index, col_index, basis_vectors, pairs)
    return to_rows.reshape(CAP), to_cols.reshape(CAP), ex, xc, vals.reshape(GROUPS, 256, 128), racc, cacc


def product_kernel(count_ref, row_at, col_at, ex, xc, vals, racc_in, cacc_in, racc, cacc):
    low, _ = lane_masks()
    lane = lax.broadcasted_iota(I32, (8, 128), 1)
    mine = [(lane // 64 == i // 2) & (lane % 2 == i % 2) for i in range(4)]
    zero = jnp.zeros((8, 128), F32)

    def rows8(ref, s):
        return pl.ds(pl.multiple_of(ref[s], 8), 8)

    def operands(s, i):
        x = xc[rows8(col_at, s), :]
        left = jnp.concatenate([jnp.where(low, x, zero), jnp.where(low, zero, x)], axis=0).astype(BF16)
        x = ex[rows8(row_at, s), :]
        other = pltpu.roll(x, 1 if i % 2 else 127, 1)
        p0, p1 = (other, x) if i % 2 else (x, other)
        right = jnp.concatenate([jnp.where(mine[i], p0, zero), jnp.where(mine[i], p1, zero)], axis=0).astype(BF16)
        return left, right

    def group(t):
        pairs = [operands(t * 8 + s, s % 4) for s in range(8)]
        left = jnp.concatenate([p[0] for p in pairs], axis=0)
        right = jnp.concatenate([p[1] for p in pairs], axis=0)
        a = vals[t]
        forward = lax.dot_general(left, a, (((1,), (1,)), ((), ())), preferred_element_type=F32)
        wide = jnp.concatenate([a[:128], a[128:]], axis=1)
        backward = lax.dot_general(right, wide, (((1,), (0,)), ((), ())), preferred_element_type=F32)
        for s in range(8):
            to_row, to_col = rows8(row_at, t * 8 + s), rows8(col_at, t * 8 + s)
            h, i, m = s // 4 * 128, s * 16, mine[s % 4]
            racc[0, to_row, :] += jnp.where(m, forward[i:i + 8, h:h + 128], zero)
            racc[1, to_row, :] += jnp.where(m, forward[i + 8:i + 16, h:h + 128], zero)
            cacc[to_col, :] += jnp.where(low, backward[i:i + 8, h:h + 128], backward[i + 8:i + 16, h:h + 128])

    def step(u, carry):
        for k in range(UNROLL):
            group(u * UNROLL + k)
        return carry

    lax.fori_loop(0, (count_ref[0] + 8 * UNROLL - 1) // (8 * UNROLL), step, 0)


def products(count, row_at, col_at, ex, xc, vals, racc, cacc):
    return pl.pallas_call(
        product_kernel,
        out_shape=(pltpu.VMEM(racc.shape, F32), pltpu.VMEM(cacc.shape, F32)),
        in_specs=[SMEM, SMEM, SMEM, VMEM, VMEM, VMEM, VMEM, VMEM],
        out_specs=(VMEM, VMEM),
        input_output_aliases={6: 0, 7: 1},
        compiler_params=pltpu.CompilerParams(vmem_limit_bytes=4 * MIB),
    )(count, row_at, col_at, ex, xc, vals, racc, cacc)


def fold_row(racc, piece, put):
    low, even = lane_masks()

    def step(i, top):
        for j in range(16):
            m = i * 16 + j
            z = []
            for p in range(2):
                e, o = racc[p, block_rows(piece * 64 + 2 * m), :], racc[p, block_rows(piece * 64 + 2 * m + 1), :]
                z.append(jnp.where(low, e, o) + pltpu.roll(jnp.where(low, o, e), 64, 1))
            w = jnp.where(even, z[1], z[0])
            y = jnp.where(even, z[0], z[1]) + jnp.where(even, pltpu.roll(w, 127, 1), pltpu.roll(w, 1, 1))
            top = jnp.maximum(top, jnp.abs(put(lane_tile(m), y)))
        return top

    return lax.fori_loop(0, 2, step, jnp.zeros((8, 128), F32))


def fold_col(cacc, piece, put):
    low, _ = lane_masks()

    def step(i, top):
        for j in range(16):
            m = i * 16 + j
            e, o = cacc[block_rows(piece * 64 + 2 * m), :], cacc[block_rows(piece * 64 + 2 * m + 1), :]
            y = jnp.where(low, e, o) + pltpu.roll(jnp.where(low, o, e), 64, 1)
            top = jnp.maximum(top, jnp.abs(put(lane_tile(m), y)))
        return top

    return lax.fori_loop(0, 2, step, jnp.zeros((8, 128), F32))


def to_wire(src, top, data, scale):
    some = top > 1e-33
    inverse = jnp.where(some, TOP / jnp.where(some, top, 1.0), 0.0)
    scale[...] = top * (1.0 / TOP)

    def step(i, carry):
        for j in range(8):
            m = i * 8 + j
            halves = [jnp.round(src[:, lane_tile(m + 16 * k)] * inverse) for k in range(2)]
            data[:, lane_tile(m)] = jnp.concatenate(halves, axis=0).astype(I32).astype(I16)
        return carry

    lax.fori_loop(0, 2, step, 0)


def add_up(put, terms, wired):
    scales = [scale[...] for _, scale in wired]

    def step(i, top):
        for j in range(4):
            m = i * 4 + j
            arrived = [data[:, lane_tile(m)].astype(I32).astype(F32) for data, _ in wired]
            for k in range(2):
                at = lane_tile(m + 16 * k)
                total = None
                for term in terms:
                    total = term[:, at] if total is None else total + term[:, at]
                for a, scale in zip(arrived, scales):
                    total = total + a[8 * k:8 * k + 8] * scale
                put(at, total)
                top = jnp.maximum(top, jnp.abs(total))
        return top

    return lax.fori_loop(0, 4, step, jnp.zeros((8, 128), F32))


def scatter_kernel(racc, cacc, out_ref, for_core, from_core, row_part, col_part, sums,
                   out_data, out_scale, in_data, in_scale, send_sem, core_sem, data_sem, scale_sem):
    place = Place()
    place.greet()
    yl, x, core, z, yh = place.yl, place.x, place.core, place.z, place.yh
    out = Sender(send_sem)

    def write(ref):
        def put(at, y):
            ref[:, at] = y
            return y
        return put

    def ship(slot, src, top, to):
        to_wire(src, top, out_data.at[slot], out_scale.at[slot])
        out.send(out_scale.at[slot], in_scale.at[slot], scale_sem.at[slot], to)
        out.send(out_data.at[slot], in_data.at[slot], data_sem.at[slot], to)

    def receive(slot):
        out.arrived(in_scale.at[slot], scale_sem.at[slot], place)
        out.arrived(in_data.at[slot], data_sem.at[slot], place)
        return in_data.at[slot], in_scale.at[slot]

    for h in (1, 0):
        y_lo = 1 - yl if h else yl
        y_hi = 1 - yh if h else yh
        for d in (2, 1, 3, 0):
            fold_row(racc, place.col_of(y_lo, (x + d) % 4, 1 - core), write(for_core.at[d, h]))
            if h and d == 2:
                place.wait_greetings()
            out.send(for_core.at[d, h], from_core.at[d, h], core_sem.at[d, h], place.sibling)
        for d in (2, 1, 3, 0):
            top = fold_col(cacc, place.row_of((z + d) % 4, y_hi), write(col_part.at[d, h]))
            if d:
                ship(6 + (d - 1) * 2 + h, col_part.at[d, h], top, place.zs[d - 1])
        for d in (2, 1, 3, 0):
            out.arrived(from_core.at[d, h], core_sem.at[d, h], place)

            def put(at, y, d=d, h=h):
                y = y + from_core[d, h, :, at]
                row_part[d, h, :, at] = y
                return y

            top = fold_row(racc, place.col_of(y_lo, (x + d) % 4, core), put)
            if d:
                ship((d - 1) * 2 + h, row_part.at[d, h], top, place.xs[d - 1])
    wired = [receive(6 + (d - 1) * 2 + 1) for d in (1, 3, 2)]
    top = add_up(write(sums.at[1]), [col_part.at[0, 1]], wired)
    ship(13, sums.at[1], top, place.y_hi)
    wired = [receive((d - 1) * 2 + 1) for d in (1, 3, 2)]
    top = add_up(write(sums.at[0]), [row_part.at[0, 1]], wired)
    ship(12, sums.at[0], top, place.y_lo)
    wired = [receive(6 + (d - 1) * 2) for d in (1, 3, 2)] + [receive((d - 1) * 2) for d in (1, 3, 2)]
    add_up(write(sums.at[2]), [row_part.at[0, 0], col_part.at[0, 0]], wired)
    wired = [receive(13), receive(12)]
    add_up(write(out_ref), [sums.at[2]], wired)
    out.finish()


def scatter(racc, cacc):
    piece, wire, lanes = (NVEC, PIECE), (2 * NVEC, PIECE // 2), (NVEC, 128)
    return pl.pallas_call(
        scatter_kernel,
        out_shape=jax.ShapeDtypeStruct(piece, F32),
        in_specs=[VMEM, VMEM],
        out_specs=VMEM,
        scratch_shapes=[
            pltpu.VMEM((4, 2) + piece, F32), pltpu.VMEM((4, 2) + piece, F32),
            pltpu.VMEM((4, 2) + piece, F32), pltpu.VMEM((4, 2) + piece, F32), pltpu.VMEM((3,) + piece, F32),
            pltpu.VMEM((14,) + wire, I16), pltpu.VMEM((14,) + lanes, F32),
            pltpu.VMEM((14,) + wire, I16), pltpu.VMEM((14,) + lanes, F32),
            pltpu.SemaphoreType.DMA((36,)),
            pltpu.SemaphoreType.DMA((4, 2)), pltpu.SemaphoreType.DMA((14,)), pltpu.SemaphoreType.DMA((14,)),
        ],
        compiler_params=pltpu.CompilerParams(collective_id=1, has_side_effects=True, vmem_limit_bytes=8 * MIB),
    )(racc, cacc)


def body(basis_vectors, block_values, blk_row, blk_col, block_count):
    count = block_count.reshape(1)
    row_at, col_at, ex, xc, vals, racc, cacc = gather(
        count, blk_row.reshape(16, 128), blk_col.reshape(16, 128), basis_vectors, block_values.reshape(CAP, BLK * BLK))
    racc, cacc = products(count, row_at, col_at, ex, xc, vals, racc, cacc)
    return scatter(racc, cacc)


def solution(mesh):
    return jax.shard_map(
        body,
        mesh=mesh,
        in_specs=(
            P(None, ("row", "col")),
            P("row", "col", None, None),
            P("row", "col", None),
            P("row", "col", None),
            P("row", "col"),
        ),
        out_specs=P(None, ("row", "col")),
        check_vma=False,
    )
```

time: 69.5 us -> 50.5 us (0.73)
  Pallas kernels: 66.8 us -> 46.7 us
  local copies, waits for them, and re-layouts: 1.5 us -> 2.88 us
    pallas_call x1, Pallas kernels: 33.6 us -> 14.4 us  [scatter(): pl.pallas_call(scatter_kernel, out_shape=jax.ShapeDtypeStruct(piece, F32)...]
    unnamed x7, local copies, waits for them, and re-layouts: 1.5 us -> 2.88 us
    pallas_call x2, Pallas kernels: 33.2 us -> 32.2 us  [the longest x1 18.9 us: gather(): pl.pallas_call(gather_kernel, out_shape=(pltpu.VMEM(((NB_ROW + 1) * 8, 12...]
where the time goes in v2:
time: 50.5 us; the launch traced here: 50.2 us
  Pallas kernels  46.7 us (92%)
  local copies, waits for them, and re-layouts  2.88 us (6%)
  between operations  0.68 us (1%)
    pallas_call x1, Pallas kernels, gather(): pl.pallas_call(gather_kernel, out_shape=(pltpu.VMEM(((NB_ROW + 1) * 8, 12...  18.9 us
    pallas_call x1, Pallas kernels, scatter(): pl.pallas_call(scatter_kernel, out_shape=jax.ShapeDtypeStruct(piece, F32)...  14.4 us
    pallas_call x1, Pallas kernels, products(): pl.pallas_call(product_kernel, out_shape=(pltpu.VMEM(racc.shape, F32), pl...  13.3 us
    unnamed x7, local copies, waits for them, and re-layouts  2.88 us

profile of v2, /device:TPU:0, one launch (start us, length us, event | category | flops | bytes accessed | tf_op | source)
XLA Modules:
  0.0 50.2 jit_solution(7750391803313816093)
XLA Ops:
  0.7 0.0 copy-start
  0.7 0.8 %copy-done = bf16[8,4096]{1,0:T(8,128)(2,1)S(1)} copy-done((bf16[8,4096]{1,0:T(8,128)(2,1)S(1)}, bf16[8,4096]{1,0:T(8,128)(2,1)}, u32[]{:S(2)}) %copy-start) | copy-done | bytes 65560
  1.5 0.0 copy-start.1
  1.5 0.7 %copy-done.1 = s32[1,1,2048]{2,1,0:T(1,128)S(1)} copy-done((s32[1,1,2048]{2,1,0:T(1,128)S(1)}, s32[1,1,2048]{2,1,0:T(1,128)}, u32[]{:S(2)}) %copy-start.1) | copy-done | bytes 8216
  2.2 0.0 copy-start.2
  2.2 0.7 %copy-done.2 = s32[1,1,2048]{2,1,0:T(1,128)S(1)} copy-done((s32[1,1,2048]{2,1,0:T(1,128)S(1)}, s32[1,1,2048]{2,1,0:T(1,128)}, u32[]{:S(2)}) %copy-start.2) | copy-done | bytes 8216
  2.9 18.9 %shard_map.55 = (f32[8200,128]{1,0:T(8,128)S(1)}, f32[4104,128]{1,0:T(8,128)S(1)}, bf16[256,4,32,2,128]{4,3,2,1,0:T(2,128)(2,1)S(1)}, f32[2,8200,128]{2,1,0:T(8,...) custom-call(s32[1]{0:T(128)} %bitcast.9.count_ref, s32[16,128]{1,0:T(8,128)S(1)} %bitcast.12, ...), custom_call_target="tpu_custom_call" | custom-call | tf_op jit(solution)/shard_map/pallas_call | solution.py:173
  21.8 13.3 %shard_map.56 = (f32[2,8200,128]{2,1,0:T(8,128)S(1)}, f32[4104,128]{1,0:T(8,128)S(1)}) custom-call(s32[1]{0:T(128)} %bitcast.10.count_ref, s32[2048]{0:T(1024)S(1)} %bitcast.14, s32[2048]{0:T(1024)S(1)} %bitcast.15, f32[8200,128]{1,0:T(8,128)S(1)} %get-tuple-element.16.ex, ...), custom_call_target="tpu_custom_call", output_to_operand_aliasing={{0}: (6, {}), {1}: (7, {})} | custom-call | tf_op jit(solution)/shard_map/pallas_call | solution.py:241
  35.1 14.4 %shard_map.57 = f32[8,4096]{1,0:T(8,128)S(1)} custom-call(f32[2,8200,128]{2,1,0:T(8,128)S(1)} %get-tuple-element.21.racc, f32[4104,128]{1,0:T(8,128)S(1)} %get-tuple-element.22.cacc), custom_call_target="tpu_custom_call" | custom-call | tf_op jit(solution)/shard_map/pallas_call | solution.py:380
  49.6 0.7 %copy.12 = f32[8,4096]{1,0:T(8,128)} copy(f32[8,4096]{1,0:T(8,128)S(1)} %shard_map.57) | data formatting | bytes 262144
Async XLA Ops:
  0.7 0.8 %copy-start = (bf16[8,4096]{1,0:T(8,128)(2,1)S(1)}, bf16[8,4096]{1,0:T(8,128)(2,1)}, u32[]{:S(2)}) copy-start(bf16[8,4096]{1,0:T(8,128)(2,1)} %x_ref.1) | copy-start | bytes 196612
  1.5 0.7 %copy-start.1 = (s32[1,1,2048]{2,1,0:T(1,128)S(1)}, s32[1,1,2048]{2,1,0:T(1,128)}, u32[]{:S(2)}) copy-start(s32[1,1,2048]{2,1,0:T(1,128)} %param.7) | copy-start | bytes 24580
  2.2 0.7 %copy-start.2 = (s32[1,1,2048]{2,1,0:T(1,128)S(1)}, s32[1,1,2048]{2,1,0:T(1,128)}, u32[]{:S(2)}) copy-start(s32[1,1,2048]{2,1,0:T(1,128)} %param.8) | copy-start | bytes 24580

commit v3 on v2

--- a/solution.py
+++ b/solution.py
@@ -14,7 +14,7 @@
 NB_ROW = 1024
 NB_COL = 512
 GROUPS = CAP // 8
-UNROLL = 32
+UNROLL = 64
 TOP = 32767.0
 F32, BF16, I16, I32 = jnp.float32, jnp.bfloat16, jnp.int16, jnp.int32
 MESH = pl.DeviceIdType.MESH
@@ -100,12 +100,19 @@
     lax.fori_loop(0, 2, step, 0)
 
 
-def gather_kernel(count_ref, row_index, col_index, x_ref, val_ref, ex, xc, vals, racc, cacc, to_rows, to_cols, rowx, colx, val_sem, send_sem, row_sem, col_sem):
+def gather_kernel(count_ref, row_in, col_in, x_in, val_ref, ex, xc, vals, racc, cacc, to_rows, to_cols,
+                  x_ref, row_index, col_index, rowx, colx, in_sem, val_sem, send_sem, row_sem, col_sem):
     place = Place()
+    small = [pltpu.make_async_copy(src, dst, in_sem.at[i]) for i, (src, dst) in enumerate(
+        [(x_in, x_ref), (row_in, row_index), (col_in, col_index)])]
+    for copy in small:
+        copy.start()
     loads = [pltpu.make_async_copy(val_ref.at[:, :, q], vals.at[:, q], val_sem.at[q]) for q in range(4)]
     for load in loads:
         load.start()
     place.greet()
+    for copy in small:
+        copy.wait()
     place.wait_greetings()
     out = Sender(send_sem)
     me_c, me_r = place.col, place.row
@@ -126,18 +133,15 @@
     ex[block_rows(NB_ROW), :] = spare
     xc[block_rows(NB_COL), :] = spare
 
-    def zero_rows(i, carry):
-        at = pl.ds(pl.multiple_of(i * 128, 128), 128)
-        racc[:, at, :] = jnp.zeros((2, 128, 128), F32)
-        return carry
-
-    lax.fori_loop(0, NB_ROW * 8 // 128, zero_rows, 0)
-
-    def zero_cols(i, carry):
-        cacc[pl.ds(pl.multiple_of(i * 128, 128), 128), :] = jnp.zeros((128, 128), F32)
-        return carry
-
-    lax.fori_loop(0, NB_COL * 8 // 128, zero_cols, 0)
+    def clear(acc, blocks):
+        def step(i, carry):
+            acc[pl.ds(pl.multiple_of(i * 256, 256), 256), :] = jnp.zeros((256, 128), F32)
+            return carry
+
+        lax.fori_loop(0, blocks * 8 // 256, step, 0)
+
+    clear(racc, NB_ROW)
+    clear(cacc, NB_COL)
 
     def take_row(slot, targets):
         out.arrived(rowx.at[slot], row_sem.at[slot], place)
@@ -176,22 +180,26 @@
             pltpu.VMEM(((NB_ROW + 1) * 8, 128), F32),
             pltpu.VMEM(((NB_COL + 1) * 8, 128), F32),
             pltpu.VMEM((GROUPS, 4, 32, 2, 128), BF16),
-            pltpu.VMEM((2, (NB_ROW + 1) * 8, 128), F32),
+            pltpu.VMEM(((NB_ROW + 1) * 8, 128), F32),
             pltpu.VMEM(((NB_COL + 1) * 8, 128), F32),
             pltpu.VMEM((16, 128), I32),
             pltpu.VMEM((16, 128), I32),
         ),
-        in_specs=[SMEM, VMEM, VMEM, VMEM, ANY],
+        in_specs=[SMEM, ANY, ANY, ANY, ANY],
         out_specs=(VMEM,) * 7,
         scratch_shapes=[
+            pltpu.VMEM((NVEC, PIECE), BF16),
+            pltpu.VMEM((16, 128), I32),
+            pltpu.VMEM((16, 128), I32),
             pltpu.VMEM((N_COL, NVEC, PIECE), BF16),
             pltpu.VMEM((N_ROW, NVEC, PIECE), BF16),
+            pltpu.SemaphoreType.DMA((3,)),
             pltpu.SemaphoreType.DMA((4,)),
             pltpu.SemaphoreType.DMA((23,)),
             pltpu.SemaphoreType.DMA((N_COL,)),
             pltpu.SemaphoreType.DMA((N_ROW,)),
         ],
-        compiler_params=pltpu.CompilerParams(collective_id=0, has_side_effects=True, vmem_limit_bytes=8 * MIB),
+        compiler_params=pltpu.CompilerParams(collective_id=0, has_side_effects=True, vmem_limit_bytes=28 * MIB),
     )(count, row_index, col_index, basis_vectors, pairs)
     return to_rows.reshape(CAP), to_cols.reshape(CAP), ex, xc, vals.reshape(GROUPS, 256, 128), racc, cacc
 
@@ -200,6 +208,7 @@
     low, _ = lane_masks()
     lane = lax.broadcasted_iota(I32, (8, 128), 1)
     mine = [(lane // 64 == i // 2) & (lane % 2 == i % 2) for i in range(4)]
+    half = [lane // 64 == i // 2 for i in range(4)]
     zero = jnp.zeros((8, 128), F32)
 
     def rows8(ref, s):
@@ -224,9 +233,10 @@
         backward = lax.dot_general(right, wide, (((1,), (0,)), ((), ())), preferred_element_type=F32)
         for s in range(8):
             to_row, to_col = rows8(row_at, t * 8 + s), rows8(col_at, t * 8 + s)
-            h, i, m = s // 4 * 128, s * 16, mine[s % 4]
-            racc[0, to_row, :] += jnp.where(m, forward[i:i + 8, h:h + 128], zero)
-            racc[1, to_row, :] += jnp.where(m, forward[i + 8:i + 16, h:h + 128], zero)
+            h, i, par = s // 4 * 128, s * 16, s % 2
+            same = forward[i + 8 * par:i + 8 * par + 8, h:h + 128]
+            other = pltpu.roll(forward[i + 8 - 8 * par:i + 16 - 8 * par, h:h + 128], 127 if par else 1, 1)
+            racc[to_row, :] += jnp.where(half[s % 4], jnp.where(mine[s % 4], same, other), zero)
             cacc[to_col, :] += jnp.where(low, backward[i:i + 8, h:h + 128], backward[i + 8:i + 16, h:h + 128])
 
     def step(u, carry):
@@ -248,31 +258,13 @@
     )(count, row_at, col_at, ex, xc, vals, racc, cacc)
 
 
-def fold_row(racc, piece, put):
-    low, even = lane_masks()
+def fold(acc, piece, put):
+    low, _ = lane_masks()
 
     def step(i, top):
         for j in range(16):
             m = i * 16 + j
-            z = []
-            for p in range(2):
-                e, o = racc[p, block_rows(piece * 64 + 2 * m), :], racc[p, block_rows(piece * 64 + 2 * m + 1), :]
-                z.append(jnp.where(low, e, o) + pltpu.roll(jnp.where(low, o, e), 64, 1))
-            w = jnp.where(even, z[1], z[0])
-            y = jnp.where(even, z[0], z[1]) + jnp.where(even, pltpu.roll(w, 127, 1), pltpu.roll(w, 1, 1))
-            top = jnp.maximum(top, jnp.abs(put(lane_tile(m), y)))
-        return top
-
-    return lax.fori_loop(0, 2, step, jnp.zeros((8, 128), F32))
-
-
-def fold_col(cacc, piece, put):
-    low, _ = lane_masks()
-
-    def step(i, top):
-        for j in range(16):
-            m = i * 16 + j
-            e, o = cacc[block_rows(piece * 64 + 2 * m), :], cacc[block_rows(piece * 64 + 2 * m + 1), :]
+            e, o = acc[block_rows(piece * 64 + 2 * m), :], acc[block_rows(piece * 64 + 2 * m + 1), :]
             y = jnp.where(low, e, o) + pltpu.roll(jnp.where(low, o, e), 64, 1)
             top = jnp.maximum(top, jnp.abs(put(lane_tile(m), y)))
         return top
@@ -339,29 +331,41 @@
         out.arrived(in_data.at[slot], data_sem.at[slot], place)
         return in_data.at[slot], in_scale.at[slot]
 
-    for h in (1, 0):
-        y_lo = 1 - yl if h else yl
-        y_hi = 1 - yh if h else yh
-        for d in (2, 1, 3, 0):
-            fold_row(racc, place.col_of(y_lo, (x + d) % 4, 1 - core), write(for_core.at[d, h]))
-            if h and d == 2:
-                place.wait_greetings()
-            out.send(for_core.at[d, h], from_core.at[d, h], core_sem.at[d, h], place.sibling)
-        for d in (2, 1, 3, 0):
-            top = fold_col(cacc, place.row_of((z + d) % 4, y_hi), write(col_part.at[d, h]))
-            if d:
-                ship(6 + (d - 1) * 2 + h, col_part.at[d, h], top, place.zs[d - 1])
-        for d in (2, 1, 3, 0):
-            out.arrived(from_core.at[d, h], core_sem.at[d, h], place)
-
-            def put(at, y, d=d, h=h):
-                y = y + from_core[d, h, :, at]
-                row_part[d, h, :, at] = y
-                return y
-
-            top = fold_row(racc, place.col_of(y_lo, (x + d) % 4, core), put)
-            if d:
-                ship((d - 1) * 2 + h, row_part.at[d, h], top, place.xs[d - 1])
+    def for_sibling(h, d):
+        fold(racc, place.col_of(1 - yl if h else yl, (x + d) % 4, 1 - core), write(for_core.at[d, h]))
+
+    def send_sibling(h, d):
+        out.send(for_core.at[d, h], from_core.at[d, h], core_sem.at[d, h], place.sibling)
+
+    def columns(h, d):
+        top = fold(cacc, place.row_of((z + d) % 4, 1 - yh if h else yh), write(col_part.at[d, h]))
+        if d:
+            ship(6 + (d - 1) * 2 + h, col_part.at[d, h], top, place.zs[d - 1])
+
+    def rows(h, d):
+        out.arrived(from_core.at[d, h], core_sem.at[d, h], place)
+
+        def put(at, y):
+            y = y + from_core[d, h, :, at]
+            row_part[d, h, :, at] = y
+            return y
+
+        top = fold(racc, place.col_of(1 - yl if h else yl, (x + d) % 4, core), put)
+        if d:
+            ship((d - 1) * 2 + h, row_part.at[d, h], top, place.xs[d - 1])
+
+    order = [(1, 2), (1, 1), (1, 3), (0, 2), (0, 1), (0, 3), (1, 0), (0, 0)]
+    for_sibling(*order[0])
+    for_sibling(*order[1])
+    place.wait_greetings()
+    send_sibling(*order[0])
+    send_sibling(*order[1])
+    for k in range(8):
+        columns(*order[k])
+        if k + 2 < 8:
+            for_sibling(*order[k + 2])
+            send_sibling(*order[k + 2])
+        rows(*order[k])
     wired = [receive(6 + (d - 1) * 2 + 1) for d in (1, 3, 2)]
     top = add_up(write(sums.at[1]), [col_part.at[0, 1]], wired)
     ship(13, sums.at[1], top, place.y_hi)

time: 50.5 us -> 47.2 us (0.935)
  local copies, waits for them, and re-layouts: 2.88 us -> 0.66 us
  Pallas kernels: 46.7 us -> 45.1 us
    unnamed x7 -> x1, local copies, waits for them, and re-layouts: 2.88 us -> 0.66 us
    pallas_call x1, Pallas kernels: 14.4 us -> 13.2 us  [scatter(): pl.pallas_call(scatter_kernel, out_shape=jax.ShapeDtypeStruct(piece, F32)...]
where the time goes in v3:
time: 47.2 us; the launch traced here: 46.4 us
  Pallas kernels  45.1 us (96%)
  between operations  0.67 us (1%)
  local copies, waits for them, and re-layouts  0.66 us (1%)
    pallas_call x1, Pallas kernels, gather(): pl.pallas_call(gather_kernel, out_shape=(pltpu.VMEM(((NB_ROW + 1) * 8, 12...  19.1 us
    pallas_call x1, Pallas kernels, scatter(): pl.pallas_call(scatter_kernel, out_shape=jax.ShapeDtypeStruct(piece, F32)...  13.2 us
    pallas_call x1, Pallas kernels, products(): pl.pallas_call(product_kernel, out_shape=(pltpu.VMEM(racc.shape, F32), pl...  12.9 us

profile of v3, /device:TPU:0, one launch (start us, length us, event | category | flops | bytes accessed | tf_op | source)
XLA Modules:
  0.0 46.4 jit_solution(3127485260850521674)
XLA Ops:
  0.7 19.1 %shard_map.55 = (f32[8200,128]{1,0:T(8,128)S(1)}, f32[4104,128]{1,0:T(8,128)S(1)}, bf16[256,4,32,2,128]{4,3,2,1,0:T(2,128)(2,1)S(1)}, f32[8200,128]{1,0:T(8,128)...) custom-call(s32[1]{0:T(128)} %bitcast.9.count_ref, s32[16,128]{1,0:T(8,128)} %bitcast.15, ...), custom_call_target="tpu_custom_call" | custom-call | tf_op jit(solution)/shard_map/pallas_call | solution.py:177
  19.7 12.9 %shard_map.56 = (f32[8200,128]{1,0:T(8,128)S(1)}, f32[4104,128]{1,0:T(8,128)S(1)}) custom-call(s32[1]{0:T(128)} %bitcast.10.count_ref, s32[2048]{0:T(1024)S(1)} %bitcast.12, s32[2048]{0:T(1024)S(1)} %bitcast.13, f32[8200,128]{1,0:T(8,128)S(1)} %get-tuple-element.16.ex, ...), custom_call_target="tpu_custom_call", output_to_operand_aliasing={{0}: (6, {}), {1}: (7, {})} | custom-call | tf_op jit(solution)/shard_map/pallas_call | solution.py:251
  32.6 13.2 %shard_map.57 = f32[8,4096]{1,0:T(8,128)S(1)} custom-call(f32[8200,128]{1,0:T(8,128)S(1)} %get-tuple-element.21.racc, f32[4104,128]{1,0:T(8,128)S(1)} %get-tuple-element.22.cacc), custom_call_target="tpu_custom_call" | custom-call | tf_op jit(solution)/shard_map/pallas_call | solution.py:384
  45.8 0.7 %copy.12 = f32[8,4096]{1,0:T(8,128)} copy(f32[8,4096]{1,0:T(8,128)S(1)} %shard_map.57) | data formatting | bytes 262144

commit v4 on v3

--- a/solution.py
+++ b/solution.py
@@ -101,10 +101,17 @@
 
 
 def gather_kernel(count_ref, row_in, col_in, x_in, val_ref, ex, xc, vals, racc, cacc, to_rows, to_cols,
-                  x_ref, row_index, col_index, rowx, colx, in_sem, val_sem, send_sem, row_sem, col_sem):
+                  row_index, col_index, rowx, colx, in_sem, val_sem, send_sem, row_sem, col_sem, core_sem):
     place = Place()
+    yl, x, core, z, yh = place.yl, place.x, place.core, place.z, place.yh
+    me_r = place.row
+
+    def file(core, yl, x):
+        return core * 8 + yl * 4 + x
+
+    mine = file(core, yl, x)
     small = [pltpu.make_async_copy(src, dst, in_sem.at[i]) for i, (src, dst) in enumerate(
-        [(x_in, x_ref), (row_in, row_index), (col_in, col_index)])]
+        [(x_in, rowx.at[mine]), (row_in, row_index), (col_in, col_index)])]
     for copy in small:
         copy.start()
     loads = [pltpu.make_async_copy(val_ref.at[:, :, q], vals.at[:, q], val_sem.at[q]) for q in range(4)]
@@ -115,16 +122,14 @@
         copy.wait()
     place.wait_greetings()
     out = Sender(send_sem)
-    me_c, me_r = place.col, place.row
-    out.send(x_ref, rowx.at[me_c], row_sem.at[me_c], place.y_lo)
-    out.send(x_ref, colx.at[me_r], col_sem.at[me_r], place.y_hi)
-    for to in place.xs:
-        out.send(x_ref, rowx.at[me_c], row_sem.at[me_c], to)
-    for to in place.zs:
-        out.send(x_ref, colx.at[me_r], col_sem.at[me_r], to)
-    out.send(x_ref, rowx.at[me_c], row_sem.at[me_c], place.sibling)
-    expand(x_ref, ex, me_c)
-    expand(x_ref, xc, me_r)
+    own = rowx.at[mine]
+    out.send(own, rowx.at[mine], row_sem.at[mine], place.y_lo)
+    out.send(own, colx.at[me_r], col_sem.at[me_r], place.y_hi)
+    for d in (0, 2, 1):
+        out.send(own, rowx.at[mine], row_sem.at[mine], place.xs[d])
+        out.send(own, colx.at[me_r], col_sem.at[me_r], place.zs[d])
+    expand(own, ex, place.col)
+    expand(own, xc, me_r)
     slot = lax.broadcasted_iota(I32, (16, 128), 0) * 128 + lax.broadcasted_iota(I32, (16, 128), 1)
     used = slot < count_ref[0]
     to_rows[...] = jnp.where(used, row_index[...], NB_ROW) * 8
@@ -143,30 +148,52 @@
     clear(racc, NB_ROW)
     clear(cacc, NB_COL)
 
-    def take_row(slot, targets):
-        out.arrived(rowx.at[slot], row_sem.at[slot], place)
+    def take_row(y, d, targets):
+        at = file(core, y, (x + d) % 4)
+        out.arrived(rowx.at[at], row_sem.at[at], place)
         for to in targets:
-            out.send(rowx.at[slot], rowx.at[slot], row_sem.at[slot], to)
-        expand(rowx.at[slot], ex, slot)
+            out.send(rowx.at[at], rowx.at[at], row_sem.at[at], to)
 
     def take_col(slot, targets):
         out.arrived(colx.at[slot], col_sem.at[slot], place)
         for to in targets:
             out.send(colx.at[slot], colx.at[slot], col_sem.at[slot], to)
-        expand(colx.at[slot], xc, slot)
-
-    yl, x, core, z, yh = place.yl, place.x, place.core, place.z, place.yh
-    take_row(place.y_lo[1], place.xs + [place.sibling])
-    take_col(place.y_hi[0], place.zs)
-    for d in (1, 3, 2):
-        take_row(place.col_of(yl, (x + d) % 4, core), [place.sibling])
+
+    def four(c, y):
+        return rowx.at[pl.ds(file(c, y, 0), 4)]
+
+    def give(y):
+        out.send(four(core, y), four(core, y), core_sem.at[y], place.sibling)
+
+    def expand_row(c, y, d):
+        expand(rowx.at[file(c, y, (x + d) % 4)], ex, place.col_of(y, (x + d) % 4, c))
+
+    take_row(1 - yl, 0, [place.xs[0], place.xs[2], place.xs[1]])
+    take_col(place.row_of(z, 1 - yh), [place.zs[0], place.zs[2], place.zs[1]])
+    for d in (1, 3, 2):
+        take_row(yl, d, [])
+    give(yl)
+    expand_row(core, 1 - yl, 0)
+    expand(colx.at[place.row_of(z, 1 - yh)], xc, place.row_of(z, 1 - yh))
+    for d in (1, 3, 2):
+        expand_row(core, yl, d)
+    for d in (1, 3, 2):
         take_col(place.row_of((z + d) % 4, yh), [])
-    for d in (1, 3, 2):
-        take_row(place.col_of(1 - yl, (x + d) % 4, core), [place.sibling])
+        expand(colx.at[place.row_of((z + d) % 4, yh)], xc, place.row_of((z + d) % 4, yh))
+    for d in (1, 3, 2):
+        take_row(1 - yl, d, [])
+    give(1 - yl)
+    out.arrived(four(1 - core, yl), core_sem.at[yl], place)
+    for d in (0, 1, 2, 3):
+        expand_row(1 - core, yl, d)
+    for d in (1, 3, 2):
+        expand_row(core, 1 - yl, d)
+    for d in (1, 3, 2):
         take_col(place.row_of((z + d) % 4, 1 - yh), [])
-    for d in (0, 1, 3, 2):
-        take_row(place.col_of(yl, (x + d) % 4, 1 - core), [])
-        take_row(place.col_of(1 - yl, (x + d) % 4, 1 - core), [])
+        expand(colx.at[place.row_of((z + d) % 4, 1 - yh)], xc, place.row_of((z + d) % 4, 1 - yh))
+    out.arrived(four(1 - core, 1 - yl), core_sem.at[1 - yl], place)
+    for d in (0, 1, 2, 3):
+        expand_row(1 - core, 1 - yl, d)
     out.finish()
     for load in loads:
         load.wait()
@@ -188,16 +215,16 @@
         in_specs=[SMEM, ANY, ANY, ANY, ANY],
         out_specs=(VMEM,) * 7,
         scratch_shapes=[
-            pltpu.VMEM((NVEC, PIECE), BF16),
             pltpu.VMEM((16, 128), I32),
             pltpu.VMEM((16, 128), I32),
             pltpu.VMEM((N_COL, NVEC, PIECE), BF16),
             pltpu.VMEM((N_ROW, NVEC, PIECE), BF16),
             pltpu.SemaphoreType.DMA((3,)),
             pltpu.SemaphoreType.DMA((4,)),
-            pltpu.SemaphoreType.DMA((23,)),
+            pltpu.SemaphoreType.DMA((16,)),
             pltpu.SemaphoreType.DMA((N_COL,)),
             pltpu.SemaphoreType.DMA((N_ROW,)),
+            pltpu.SemaphoreType.DMA((2,)),
         ],
         compiler_params=pltpu.CompilerParams(collective_id=0, has_side_effects=True, vmem_limit_bytes=28 * MIB),
     )(count, row_index, col_index, basis_vectors, pairs)
@@ -272,28 +299,33 @@
     return lax.fori_loop(0, 2, step, jnp.zeros((8, 128), F32))
 
 
-def to_wire(src, top, data, scale):
+def scale_of(code):
+    return jnp.exp2(code * (1.0 / 256.0))
+
+
+def to_wire(src, top, wire):
     some = top > 1e-33
-    inverse = jnp.where(some, TOP / jnp.where(some, top, 1.0), 0.0)
-    scale[...] = top * (1.0 / TOP)
+    code = jnp.ceil(jnp.log2(jnp.where(some, top, 1.0)) * 256.0) + 1.0
+    inverse = jnp.where(some, TOP / scale_of(code), 0.0)
+    wire[:, lane_tile(16)] = jnp.concatenate([code, code], axis=0).astype(I32).astype(I16)
 
     def step(i, carry):
         for j in range(8):
             m = i * 8 + j
             halves = [jnp.round(src[:, lane_tile(m + 16 * k)] * inverse) for k in range(2)]
-            data[:, lane_tile(m)] = jnp.concatenate(halves, axis=0).astype(I32).astype(I16)
+            wire[:, lane_tile(m)] = jnp.concatenate(halves, axis=0).astype(I32).astype(I16)
         return carry
 
     lax.fori_loop(0, 2, step, 0)
 
 
-def add_up(put, terms, wired):
-    scales = [scale[...] for _, scale in wired]
+def add_up(put, terms, wires):
+    scales = [scale_of(wire[:, lane_tile(16)].astype(I32).astype(F32)[:8]) * (1.0 / TOP) for wire in wires]
 
     def step(i, top):
         for j in range(4):
             m = i * 4 + j
-            arrived = [data[:, lane_tile(m)].astype(I32).astype(F32) for data, _ in wired]
+            arrived = [wire[:, lane_tile(m)].astype(I32).astype(F32) for wire in wires]
             for k in range(2):
                 at = lane_tile(m + 16 * k)
                 total = None
@@ -309,7 +341,7 @@
 
 
 def scatter_kernel(racc, cacc, out_ref, for_core, from_core, row_part, col_part, sums,
-                   out_data, out_scale, in_data, in_scale, send_sem, core_sem, data_sem, scale_sem):
+                   out_wire, in_wire, send_sem, core_sem, wire_sem):
     place = Place()
     place.greet()
     yl, x, core, z, yh = place.yl, place.x, place.core, place.z, place.yh
@@ -321,78 +353,88 @@
             return y
         return put
 
-    def ship(slot, src, top, to):
-        to_wire(src, top, out_data.at[slot], out_scale.at[slot])
-        out.send(out_scale.at[slot], in_scale.at[slot], scale_sem.at[slot], to)
-        out.send(out_data.at[slot], in_data.at[slot], data_sem.at[slot], to)
-
-    def receive(slot):
-        out.arrived(in_scale.at[slot], scale_sem.at[slot], place)
-        out.arrived(in_data.at[slot], data_sem.at[slot], place)
-        return in_data.at[slot], in_scale.at[slot]
-
-    def for_sibling(h, d):
-        fold(racc, place.col_of(1 - yl if h else yl, (x + d) % 4, 1 - core), write(for_core.at[d, h]))
-
-    def send_sibling(h, d):
-        out.send(for_core.at[d, h], from_core.at[d, h], core_sem.at[d, h], place.sibling)
-
-    def columns(h, d):
+    def ship(at, to):
+        out.send(out_wire.at[at], in_wire.at[at], wire_sem.at[at], to)
+
+    def receive(at):
+        out.arrived(in_wire.at[at], wire_sem.at[at], place)
+
+    order = [(1, 2), (1, 1), (1, 3), (0, 2), (0, 1), (0, 3), (1, 0), (0, 0)]
+
+    def for_sibling(k):
+        h, d = order[k]
+        fold(racc, place.col_of(1 - yl if h else yl, (x + d) % 4, 1 - core), write(for_core.at[k]))
+
+    def send_sibling(k):
+        out.send(for_core.at[k], from_core.at[k], core_sem.at[k], place.sibling)
+
+    def columns(k):
+        h, d = order[k]
+        at = 6 + (d - 1) * 2 + h
         top = fold(cacc, place.row_of((z + d) % 4, 1 - yh if h else yh), write(col_part.at[d, h]))
         if d:
-            ship(6 + (d - 1) * 2 + h, col_part.at[d, h], top, place.zs[d - 1])
-
-    def rows(h, d):
-        out.arrived(from_core.at[d, h], core_sem.at[d, h], place)
+            to_wire(col_part.at[d, h], top, out_wire.at[at])
+            ship(at, place.zs[d - 1])
+
+    def rows(k):
+        h, d = order[k]
+        out.arrived(from_core.at[k], core_sem.at[k], place)
 
         def put(at, y):
-            y = y + from_core[d, h, :, at]
+            y = y + from_core[k, :, at]
             row_part[d, h, :, at] = y
             return y
 
         top = fold(racc, place.col_of(1 - yl if h else yl, (x + d) % 4, core), put)
         if d:
-            ship((d - 1) * 2 + h, row_part.at[d, h], top, place.xs[d - 1])
-
-    order = [(1, 2), (1, 1), (1, 3), (0, 2), (0, 1), (0, 3), (1, 0), (0, 0)]
-    for_sibling(*order[0])
-    for_sibling(*order[1])
+            to_wire(row_part.at[d, h], top, out_wire.at[(d - 1) * 2 + h])
+            ship((d - 1) * 2 + h, place.xs[d - 1])
+
+    for_sibling(0)
+    for_sibling(1)
     place.wait_greetings()
-    send_sibling(*order[0])
-    send_sibling(*order[1])
+    send_sibling(0)
+    send_sibling(1)
     for k in range(8):
-        columns(*order[k])
+        columns(k)
         if k + 2 < 8:
-            for_sibling(*order[k + 2])
-            send_sibling(*order[k + 2])
-        rows(*order[k])
-    wired = [receive(6 + (d - 1) * 2 + 1) for d in (1, 3, 2)]
-    top = add_up(write(sums.at[1]), [col_part.at[0, 1]], wired)
-    ship(13, sums.at[1], top, place.y_hi)
-    wired = [receive((d - 1) * 2 + 1) for d in (1, 3, 2)]
-    top = add_up(write(sums.at[0]), [row_part.at[0, 1]], wired)
-    ship(12, sums.at[0], top, place.y_lo)
-    wired = [receive(6 + (d - 1) * 2) for d in (1, 3, 2)] + [receive((d - 1) * 2) for d in (1, 3, 2)]
-    add_up(write(sums.at[2]), [row_part.at[0, 0], col_part.at[0, 0]], wired)
-    wired = [receive(13), receive(12)]
-    add_up(write(out_ref), [sums.at[2]], wired)
+            for_sibling(k + 2)
+            send_sibling(k + 2)
+        rows(k)
+    for d in (1, 3, 2):
+        receive(6 + (d - 1) * 2 + 1)
+    top = add_up(write(sums.at[1]), [col_part.at[0, 1]], [in_wire.at[6 + (d - 1) * 2 + 1] for d in (1, 3, 2)])
+    to_wire(sums.at[1], top, out_wire.at[13])
+    ship(13, place.y_hi)
+    for d in (1, 3, 2):
+        receive((d - 1) * 2 + 1)
+    top = add_up(write(sums.at[0]), [row_part.at[0, 1]], [in_wire.at[(d - 1) * 2 + 1] for d in (1, 3, 2)])
+    to_wire(sums.at[0], top, out_wire.at[12])
+    ship(12, place.y_lo)
+    for d in (1, 3, 2):
+        receive((d - 1) * 2)
+        receive(6 + (d - 1) * 2)
+    add_up(write(sums.at[2]), [row_part.at[0, 0], col_part.at[0, 0]],
+           [in_wire.at[(d - 1) * 2] for d in (1, 3, 2)] + [in_wire.at[6 + (d - 1) * 2] for d in (1, 3, 2)])
+    receive(13)
+    receive(12)
+    add_up(write(out_ref), [sums.at[2]], [in_wire.at[13], in_wire.at[12]])
     out.finish()
 
 
 def scatter(racc, cacc):
-    piece, wire, lanes = (NVEC, PIECE), (2 * NVEC, PIECE // 2), (NVEC, 128)
+    piece, wire = (NVEC, PIECE), (2 * NVEC, PIECE // 2 + 128)
     return pl.pallas_call(
         scatter_kernel,
         out_shape=jax.ShapeDtypeStruct(piece, F32),
         in_specs=[VMEM, VMEM],
         out_specs=VMEM,
         scratch_shapes=[
-            pltpu.VMEM((4, 2) + piece, F32), pltpu.VMEM((4, 2) + piece, F32),
+            pltpu.VMEM((8,) + piece, F32), pltpu.VMEM((8,) + piece, F32),
             pltpu.VMEM((4, 2) + piece, F32), pltpu.VMEM((4, 2) + piece, F32), pltpu.VMEM((3,) + piece, F32),
-            pltpu.VMEM((14,) + wire, I16), pltpu.VMEM((14,) + lanes, F32),
-            pltpu.VMEM((14,) + wire, I16), pltpu.VMEM((14,) + lanes, F32),
-            pltpu.SemaphoreType.DMA((36,)),
-            pltpu.SemaphoreType.DMA((4, 2)), pltpu.SemaphoreType.DMA((14,)), pltpu.SemaphoreType.DMA((14,)),
+            pltpu.VMEM((14,) + wire, I16), pltpu.VMEM((14,) + wire, I16),
+            pltpu.SemaphoreType.DMA((22,)),
+            pltpu.SemaphoreType.DMA((8,)), pltpu.SemaphoreType.DMA((14,)),
         ],
         compiler_params=pltpu.CompilerParams(collective_id=1, has_side_effects=True, vmem_limit_bytes=8 * MIB),
     )(racc, cacc)

time: 47.2 us -> 46.2 us (0.979)
  Pallas kernels: 45.1 us -> 44 us
    pallas_call x1, Pallas kernels: 19.1 us -> 18.1 us  [gather(): pl.pallas_call(gather_kernel, out_shape=(pltpu.VMEM(((NB_ROW + 1) * 8, 12...]
where the time goes in v4:
time: 46.2 us; the launch traced here: 45.3 us
  Pallas kernels  44 us (95%)
  between operations  0.67 us (1%)
  local copies, waits for them, and re-layouts  0.66 us (1%)
    pallas_call x1, Pallas kernels, gather(): pl.pallas_call(gather_kernel, out_shape=(pltpu.VMEM(((NB_ROW + 1) * 8, 12...  18.1 us
    pallas_call x1, Pallas kernels, scatter(): pl.pallas_call(scatter_kernel, out_shape=jax.ShapeDtypeStruct(piece, F32)...  12.9 us
    pallas_call x1, Pallas kernels, products(): pl.pallas_call(product_kernel, out_shape=(pltpu.VMEM(racc.shape, F32), pl...  12.9 us

profile of v4, /device:TPU:0, one launch (start us, length us, event | category | flops | bytes accessed | tf_op | source)
XLA Modules:
  0.0 45.3 jit_solution(4642766815758982987)
XLA Ops:
  0.7 18.1 %shard_map.55 = (f32[8200,128]{1,0:T(8,128)S(1)}, f32[4104,128]{1,0:T(8,128)S(1)}, bf16[256,4,32,2,128]{4,3,2,1,0:T(2,128)(2,1)S(1)}, f32[8200,128]{1,0:T(8,128)...) custom-call(s32[1]{0:T(128)} %bitcast.9.count_ref, s32[16,128]{1,0:T(8,128)} %bitcast.15, ...), custom_call_target="tpu_custom_call" | custom-call | tf_op jit(solution)/shard_map/pallas_call | solution.py:204
  18.8 12.9 %shard_map.56 = (f32[8200,128]{1,0:T(8,128)S(1)}, f32[4104,128]{1,0:T(8,128)S(1)}) custom-call(s32[1]{0:T(128)} %bitcast.10.count_ref, s32[2048]{0:T(1024)S(1)} %bitcast.12, s32[2048]{0:T(1024)S(1)} %bitcast.13, f32[8200,128]{1,0:T(8,128)S(1)} %get-tuple-element.16.ex, ...), custom_call_target="tpu_custom_call", output_to_operand_aliasing={{0}: (6, {}), {1}: (7, {})} | custom-call | tf_op jit(solution)/shard_map/pallas_call | solution.py:278
  31.7 12.9 %shard_map.57 = f32[8,4096]{1,0:T(8,128)S(1)} custom-call(f32[8200,128]{1,0:T(8,128)S(1)} %get-tuple-element.21.racc, f32[4104,128]{1,0:T(8,128)S(1)} %get-tuple-element.22.cacc), custom_call_target="tpu_custom_call" | custom-call | tf_op jit(solution)/shard_map/pallas_call | solution.py:427
  44.7 0.7 %copy.12 = f32[8,4096]{1,0:T(8,128)} copy(f32[8,4096]{1,0:T(8,128)S(1)} %shard_map.57) | data formatting | bytes 262144

commit v5 on v4

--- a/solution.py
+++ b/solution.py
@@ -14,7 +14,7 @@
 NB_ROW = 1024
 NB_COL = 512
 GROUPS = CAP // 8
-UNROLL = 64
+UNROLL = 128
 TOP = 32767.0
 F32, BF16, I16, I32 = jnp.float32, jnp.bfloat16, jnp.int16, jnp.int32
 MESH = pl.DeviceIdType.MESH
@@ -345,7 +345,6 @@
     place = Place()
     place.greet()
     yl, x, core, z, yh = place.yl, place.x, place.core, place.z, place.yh
-    out = Sender(send_sem)
 
     def write(ref):
         def put(at, y):
@@ -353,64 +352,79 @@
             return y
         return put
 
-    def ship(at, to):
-        out.send(out_wire.at[at], in_wire.at[at], wire_sem.at[at], to)
+    def remote(src, dst, sem, recv_sem, to):
+        return pltpu.make_async_remote_copy(
+            src_ref=src, dst_ref=dst, send_sem=send_sem.at[sem], recv_sem=recv_sem, device_id=to, device_id_type=MESH)
+
+    def wire(at, to):
+        return remote(out_wire.at[at], in_wire.at[at], at, wire_sem.at[at], to)
+
+    def core_copy(k):
+        return remote(for_core.at[k], from_core.at[k], 14 + k, core_sem.at[k], place.sibling)
 
     def receive(at):
-        out.arrived(in_wire.at[at], wire_sem.at[at], place)
-
-    order = [(1, 2), (1, 1), (1, 3), (0, 2), (0, 1), (0, 3), (1, 0), (0, 0)]
+        wire(at, place.sibling).wait_recv()
+
+    def order(k):
+        last, j = k // 6, k % 3
+        return (1 - last) * (1 - k // 3) + last * (7 - k), (1 - last) * (2 - j + 3 * (j // 2))
 
     def for_sibling(k):
-        h, d = order[k]
-        fold(racc, place.col_of(1 - yl if h else yl, (x + d) % 4, 1 - core), write(for_core.at[k]))
-
-    def send_sibling(k):
-        out.send(for_core.at[k], from_core.at[k], core_sem.at[k], place.sibling)
+        h, d = order(k)
+        fold(racc, place.col_of(h * (1 - yl) + (1 - h) * yl, (x + d) % 4, 1 - core), write(for_core.at[k]))
 
     def columns(k):
-        h, d = order[k]
-        at = 6 + (d - 1) * 2 + h
-        top = fold(cacc, place.row_of((z + d) % 4, 1 - yh if h else yh), write(col_part.at[d, h]))
-        if d:
-            to_wire(col_part.at[d, h], top, out_wire.at[at])
-            ship(at, place.zs[d - 1])
+        h, d = order(k)
+        return h, d, fold(cacc, place.row_of((z + d) % 4, h * (1 - yh) + (1 - h) * yh), write(col_part.at[d, h]))
 
     def rows(k):
-        h, d = order[k]
-        out.arrived(from_core.at[k], core_sem.at[k], place)
+        h, d = order(k)
+        core_copy(k).wait_recv()
 
         def put(at, y):
             y = y + from_core[k, :, at]
             row_part[d, h, :, at] = y
             return y
 
-        top = fold(racc, place.col_of(1 - yl if h else yl, (x + d) % 4, core), put)
-        if d:
-            to_wire(row_part.at[d, h], top, out_wire.at[(d - 1) * 2 + h])
-            ship((d - 1) * 2 + h, place.xs[d - 1])
+        return h, d, fold(racc, place.col_of(h * (1 - yl) + (1 - h) * yl, (x + d) % 4, core), put)
 
     for_sibling(0)
+    place.wait_greetings()
+    core_copy(0).start()
     for_sibling(1)
-    place.wait_greetings()
-    send_sibling(0)
-    send_sibling(1)
-    for k in range(8):
+    core_copy(1).start()
+
+    def each(k, carry):
+        h, d, top = columns(k)
+        at = 6 + (d - 1) * 2 + h
+        to_wire(col_part.at[d, h], top, out_wire.at[at])
+        wire(at, (place.row_of((z + d) % 4, yh), place.col)).start()
+        for_sibling(k + 2)
+        core_copy(k + 2).start()
+        h, d, top = rows(k)
+        at = (d - 1) * 2 + h
+        to_wire(row_part.at[d, h], top, out_wire.at[at])
+        wire(at, (place.row, place.col_of(yl, (x + d) % 4, core))).start()
+        return carry
+
+    lax.fori_loop(0, 6, each, 0)
+
+    def keep(k, carry):
         columns(k)
-        if k + 2 < 8:
-            for_sibling(k + 2)
-            send_sibling(k + 2)
         rows(k)
+        return carry
+
+    lax.fori_loop(6, 8, keep, 0)
     for d in (1, 3, 2):
         receive(6 + (d - 1) * 2 + 1)
     top = add_up(write(sums.at[1]), [col_part.at[0, 1]], [in_wire.at[6 + (d - 1) * 2 + 1] for d in (1, 3, 2)])
     to_wire(sums.at[1], top, out_wire.at[13])
-    ship(13, place.y_hi)
+    wire(13, place.y_hi).start()
     for d in (1, 3, 2):
         receive((d - 1) * 2 + 1)
     top = add_up(write(sums.at[0]), [row_part.at[0, 1]], [in_wire.at[(d - 1) * 2 + 1] for d in (1, 3, 2)])
     to_wire(sums.at[0], top, out_wire.at[12])
-    ship(12, place.y_lo)
+    wire(12, place.y_lo).start()
     for d in (1, 3, 2):
         receive((d - 1) * 2)
         receive(6 + (d - 1) * 2)
@@ -419,7 +433,17 @@
     receive(13)
     receive(12)
     add_up(write(out_ref), [sums.at[2]], [in_wire.at[13], in_wire.at[12]])
-    out.finish()
+
+    def sent_wire(at, carry):
+        wire(at, place.sibling).wait_send()
+        return carry
+
+    def sent_core(k, carry):
+        core_copy(k).wait_send()
+        return carry
+
+    lax.fori_loop(0, 14, sent_wire, 0)
+    lax.fori_loop(0, 8, sent_core, 0)
 
 
 def scatter(racc, cacc):

time: 46.2 us -> 47.1 us (1.019)
  Pallas kernels: 44 us -> 45.2 us
    pallas_call x1, Pallas kernels: 12.9 us -> 19.2 us  [scatter(): pl.pallas_call(scatter_kernel, out_shape=jax.ShapeDtypeStruct(piece, F32)...]
    pallas_call x1, Pallas kernels: 12.9 us -> 7.87 us  [products(): pl.pallas_call(product_kernel, out_shape=(pltpu.VMEM(racc.shape, F32), pl...]
where the time goes in v5:
time: 47.1 us; the launch traced here: 46.5 us
  Pallas kernels  45.2 us (96%)
  between operations  0.67 us (1%)
  local copies, waits for them, and re-layouts  0.66 us (1%)
    pallas_call x1, Pallas kernels, scatter(): pl.pallas_call(scatter_kernel, out_shape=jax.ShapeDtypeStruct(piece, F32)...  19.2 us
    pallas_call x1, Pallas kernels, gather(): pl.pallas_call(gather_kernel, out_shape=(pltpu.VMEM(((NB_ROW + 1) * 8, 12...  18.1 us
    pallas_call x1, Pallas kernels, products(): pl.pallas_call(product_kernel, out_shape=(pltpu.VMEM(racc.shape, F32), pl...  7.87 us

profile of v5, /device:TPU:0, one launch (start us, length us, event | category | flops | bytes accessed | tf_op | source)
XLA Modules:
  0.0 46.5 jit_solution(845520643228378452)
XLA Ops:
  0.7 18.1 %shard_map.55 = (f32[8200,128]{1,0:T(8,128)S(1)}, f32[4104,128]{1,0:T(8,128)S(1)}, bf16[256,4,32,2,128]{4,3,2,1,0:T(2,128)(2,1)S(1)}, f32[8200,128]{1,0:T(8,128)...) custom-call(s32[1]{0:T(128)} %bitcast.9.count_ref, s32[16,128]{1,0:T(8,128)} %bitcast.15, ...), custom_call_target="tpu_custom_call" | custom-call | tf_op jit(solution)/shard_map/pallas_call | solution.py:204
  18.8 7.9 %shard_map.56 = (f32[8200,128]{1,0:T(8,128)S(1)}, f32[4104,128]{1,0:T(8,128)S(1)}) custom-call(s32[1]{0:T(128)} %bitcast.10.count_ref, s32[2048]{0:T(1024)S(1)} %bitcast.12, s32[2048]{0:T(1024)S(1)} %bitcast.13, f32[8200,128]{1,0:T(8,128)S(1)} %get-tuple-element.16.ex, ...), custom_call_target="tpu_custom_call", output_to_operand_aliasing={{0}: (6, {}), {1}: (7, {})} | custom-call | tf_op jit(solution)/shard_map/pallas_call | solution.py:278
  26.7 19.2 %shard_map.57 = f32[8,4096]{1,0:T(8,128)S(1)} custom-call(f32[8200,128]{1,0:T(8,128)S(1)} %get-tuple-element.21.racc, f32[4104,128]{1,0:T(8,128)S(1)} %get-tuple-element.22.cacc), custom_call_target="tpu_custom_call" | custom-call | tf_op jit(solution)/shard_map/pallas_call | solution.py:451
  45.8 0.7 %copy.12 = f32[8,4096]{1,0:T(8,128)} copy(f32[8,4096]{1,0:T(8,128)S(1)} %shard_map.57) | data formatting | bytes 262144
